TPU v7x, 32 devices: a whole 2x2x4 slice. The times are simulated.
32 devices in a mesh: det: 4 (over y, core), tm: 8 (over z, x).
Axes of the slice: x: 2, y: 2, z: 4, core: 2. Of those that a mesh axis runs over, the one named last changes fastest.
Arguments:
- detector_data: float32 [256, 65536], P('det', 'tm'), may hold values from -6 to 6
- sky_map: float32 [4096, 8192], P(('det', 'tm')), may hold values from -6 to 6
- pointing: int32 [256, 512], P('det', 'tm'), may hold values from 0 to 2047
- request_owner: int32 [512, 1], P(('det', 'tm')), may hold values from 0 to 7; in each aligned block of 16 rows (0 to 15, 16 to 31, ...) at most 4 rows name the same one
- request_block: int32 [512], P(('det', 'tm')), may hold values from 0 to 63
- beam_kernel: float32 [128, 128], replicated, may hold values from -0.5 to 0.5
- inv_white: float32 [256, 32], P('det'), may hold values from 0.5 to 4
- mode_loading: float32 [256, 16], P('det'), may hold values from -1.5 to 1.5
- mode_kernel: float32 [32, 16, 16], replicated, may hold values from -0.75 to 0.75
Outputs:
- map_gradient: float32 [4096, 8192], P(('det', 'tm'))
Inputs may be any that keep to these rules, and one draw needn't show every extreme that they name: `request_owner`: among the 16 requests of one device, no owner is named more than 4 times, and in every draw some device names some owner exactly 4 times.
All inputs are finite; a program needn't handle non-finite values.
Results may differ from a plain program's by a relative error of at most 0.0003.
Values sent between devices are 32-bit elements; how exact they have to be, the bound alone decides.
A program may use at most 256 MiB of HBM per device.

v0:
```python
import math

import jax
import jax.numpy as jnp
from jax import lax
from jax.sharding import PartitionSpec as P

TA = 64
NBAND = 32
BANDW = 128
XA = 64
YA = 64


precise = lax.Precision.HIGHEST


def twiddle_table(rows_count, cols_count, modulus, direction):
    left_index = jnp.arange(rows_count, dtype=jnp.int32)[:, None]
    right_index = jnp.arange(cols_count, dtype=jnp.int32)[None, :]
    phase_angle = (left_index * right_index % modulus).astype(jnp.float32) * (
        2.0 * math.pi / modulus
    )
    return (jnp.cos(phase_angle), direction * jnp.sin(phase_angle))


def transform_last(real_part, imag_part, first_factor, second_factor, direction, real_only):
    length = first_factor * second_factor
    leading = real_part.shape[:-1]
    shaped_real = real_part.reshape(leading + (first_factor, second_factor))
    outer_real, outer_imag = twiddle_table(first_factor, first_factor, first_factor, direction)
    section_real = jnp.einsum("ka,...ab->...kb", outer_real, shaped_real, precision=precise)
    section_imag = jnp.einsum("ka,...ab->...kb", outer_imag, shaped_real, precision=precise)
    if imag_part is not None:
        shaped_imag = imag_part.reshape(leading + (first_factor, second_factor))
        section_real = section_real - jnp.einsum(
            "ka,...ab->...kb", outer_imag, shaped_imag, precision=precise
        )
        section_imag = section_imag + jnp.einsum(
            "ka,...ab->...kb", outer_real, shaped_imag, precision=precise
        )
    twist_real, twist_imag = twiddle_table(first_factor, second_factor, length, direction)
    turned_real = section_real * twist_real - section_imag * twist_imag
    turned_imag = section_real * twist_imag + section_imag * twist_real
    inner_real, inner_imag = twiddle_table(second_factor, second_factor, second_factor, direction)
    final_real = jnp.einsum("qb,...kb->...qk", inner_real, turned_real, precision=precise)
    final_real = final_real - jnp.einsum(
        "qb,...kb->...qk", inner_imag, turned_imag, precision=precise
    )
    final_real = final_real.reshape(leading + (length,))
    if real_only:
        return (final_real, None)
    final_imag = jnp.einsum("qb,...kb->...qk", inner_real, turned_imag, precision=precise)
    final_imag = final_imag + jnp.einsum(
        "qb,...kb->...qk", inner_imag, turned_real, precision=precise
    )
    return (final_real, final_imag.reshape(leading + (length,)))


def prior_gain(vertical, horizontal, total_rows, total_cols):
    fold_rows = jnp.minimum(vertical, total_rows - vertical).astype(jnp.float32) / total_rows
    fold_cols = jnp.minimum(horizontal, total_cols - horizontal).astype(jnp.float32) / total_cols
    radial_sq = fold_rows * fold_rows + fold_cols * fold_cols
    length_scale = total_rows / 64.0
    knee_sq = 1.0 / (2.0 * math.pi * length_scale) ** 2
    return 1.0 + radial_sq / 0.05 + 0.25 / jnp.sqrt(radial_sq + knee_sq)


def couple_modes(projection, kernel, band_onehot):
    kernel_freq = jnp.einsum("bmn,bf->mnf", kernel, band_onehot, precision=precise)
    return jnp.einsum("mnf,cnf->cmf", kernel_freq, projection, precision=precise)


def local(
    detector_data,
    sky_map,
    pointing,
    request_owner,
    request_block,
    beam_kernel,
    inv_white,
    mode_loading,
    mode_kernel,
):
    det_rows, samples = detector_data.shape
    rows_here, map_cols = sky_map.shape
    det_count = lax.axis_size("det")
    owners = lax.axis_size("tm")
    devices = det_count * owners
    tile_width = beam_kernel.shape[0]
    blocks_here = map_cols // tile_width
    wanted = request_owner.shape[0]
    capacity = max(2, 2 * wanted // owners)
    target = request_owner[:, 0]
    onehot_owner = (target[:, None] == jnp.arange(owners, dtype=jnp.int32)[None, :]).astype(
        jnp.int32
    )
    position = jnp.sum((jnp.cumsum(onehot_owner, axis=0) - 1) * onehot_owner, axis=1)
    slot_index = target * capacity + position
    send_ids = (
        jnp.full((owners * capacity,), blocks_here, jnp.int32).at[slot_index].set(request_block)
    )
    asked_ids = lax.all_to_all(
        send_ids.reshape(owners, capacity), "tm", split_axis=0, concat_axis=0, tiled=True
    )
    stored = sky_map.reshape(rows_here, blocks_here, tile_width).transpose(1, 0, 2)
    outgoing = jnp.take(stored, asked_ids, axis=0, mode="clip")
    arrived = lax.all_to_all(outgoing, "tm", split_axis=0, concat_axis=0, tiled=True)
    arrived_rows = arrived.reshape(owners * capacity * rows_here, tile_width)
    list_slot = pointing // rows_here
    block_row = pointing % rows_here
    row_index = (slot_index[list_slot] * rows_here + block_row).reshape(-1)
    gathered = jnp.take(arrived_rows, row_index, axis=0)
    signal = jnp.dot(gathered, beam_kernel.T, precision=precise).reshape(det_rows, samples)
    residual = detector_data - signal
    spec_real, spec_imag = transform_last(residual, None, TA, samples // TA, -1.0, False)
    frequency = jnp.arange(samples, dtype=jnp.int32)
    folded = jnp.minimum(frequency, samples - frequency)
    band_index = jnp.minimum(folded // BANDW, NBAND - 1)
    band_onehot = (jnp.arange(NBAND, dtype=jnp.int32)[:, None] == band_index[None, :]).astype(
        jnp.float32
    )
    weight_freq = jnp.dot(inv_white, band_onehot, precision=precise)
    local_proj = jnp.stack(
        [
            jnp.einsum("jm,jf->mf", mode_loading, weight_freq * spec_real, precision=precise),
            jnp.einsum("jm,jf->mf", mode_loading, weight_freq * spec_imag, precision=precise),
        ],
        axis=0,
    )
    mode_share = lax.psum_scatter(local_proj, "det", scatter_dimension=2, tiled=True)
    share_width = mode_share.shape[2]
    share_start = lax.axis_index("det") * share_width
    share_onehot = lax.dynamic_slice_in_dim(band_onehot, share_start, share_width, 1)
    coupled = lax.all_gather(
        couple_modes(mode_share, mode_kernel, share_onehot), "det", axis=2, tiled=True
    )
    filt_real = weight_freq * (
        spec_real - jnp.einsum("jm,mf->jf", mode_loading, coupled[0], precision=precise)
    )
    filt_imag = weight_freq * (
        spec_imag - jnp.einsum("jm,mf->jf", mode_loading, coupled[1], precision=precise)
    )
    cleaned, _ = transform_last(filt_real, filt_imag, TA, samples // TA, 1.0, True)
    cleaned = cleaned / samples
    row_grads = jnp.dot(cleaned.reshape(-1, tile_width), beam_kernel, precision=precise)
    returned = jnp.zeros_like(arrived_rows).at[row_index].add(row_grads)
    returned = returned.reshape(owners, capacity, rows_here, tile_width)
    delivered = lax.all_to_all(returned, "tm", split_axis=0, concat_axis=0, tiled=True)
    accumulated = jnp.zeros((blocks_here, rows_here, tile_width), jnp.float32)
    accumulated = accumulated.at[asked_ids.reshape(-1)].add(
        delivered.reshape(-1, rows_here, tile_width), mode="drop"
    )
    data_grad = accumulated.transpose(1, 0, 2).reshape(rows_here, map_cols)
    per_device = map_cols // devices
    total_rows = rows_here * devices
    row_real, row_imag = transform_last(sky_map, None, XA, map_cols // XA, -1.0, False)
    packed = jnp.stack(
        [
            row_real.reshape(rows_here, devices, per_device),
            row_imag.reshape(rows_here, devices, per_device),
        ],
        axis=2,
    )
    packed = packed.transpose(1, 0, 2, 3).reshape(devices, rows_here, 2 * per_device)
    columns = lax.all_to_all(packed, ("det", "tm"), split_axis=0, concat_axis=0, tiled=True)
    columns = columns.reshape(total_rows, 2, per_device)
    col_real = columns[:, 0, :].T
    col_imag = columns[:, 1, :].T
    full_real, full_imag = transform_last(col_real, col_imag, YA, total_rows // YA, -1.0, False)
    device_rank = lax.axis_index("det") * owners + lax.axis_index("tm")
    col_freq = device_rank * per_device + jnp.arange(per_device, dtype=jnp.int32)
    gain_grid = prior_gain(
        jnp.arange(total_rows, dtype=jnp.int32)[None, :], col_freq[:, None], total_rows, map_cols
    )
    back_real, back_imag = transform_last(
        full_real * gain_grid, full_imag * gain_grid, YA, total_rows // YA, 1.0, False
    )
    stacked = jnp.stack([back_real, back_imag], axis=0).reshape(2, per_device, devices, rows_here)
    stacked = stacked.transpose(2, 3, 0, 1).reshape(devices, rows_here, 2 * per_device)
    returned_rows = lax.all_to_all(stacked, ("det", "tm"), split_axis=0, concat_axis=0, tiled=True)
    returned_rows = returned_rows.reshape(devices, rows_here, 2, per_device)
    spec_rows_real = returned_rows[:, :, 0, :].transpose(1, 0, 2).reshape(rows_here, map_cols)
    spec_rows_imag = returned_rows[:, :, 1, :].transpose(1, 0, 2).reshape(rows_here, map_cols)
    prior_term, _ = transform_last(spec_rows_real, spec_rows_imag, XA, map_cols // XA, 1.0, True)
    prior_term = prior_term / (total_rows * map_cols)
    return data_grad - prior_term


def solution(mesh):
    return jax.shard_map(
        local,
        mesh=mesh,
        in_specs=(
            P("det", "tm"),
            P(("det", "tm"), None),
            P("det", "tm"),
            P(("det", "tm"), None),
            P(("det", "tm")),
            P(),
            P("det", None),
            P("det", None),
            P(),
        ),
        out_specs=P(("det", "tm"), None),
        check_vma=False,
    )
```

profile of v0, /device:TPU:0, one launch (start us, length us, event | category | flops | bytes accessed | tf_op | source)
XLA Modules:
  0.0 789.7 jit_solution(2940725415999710479)
XLA Ops:
  10.3 7.3 all-to-all-start
  17.5 5.6 copy.116
  23.1 5.6 copy.117
  28.8 4.2 gather_fusion.1
  33.0 6.0 all-to-all-start.1
  39.0 5.4 copy.125
  44.6 6.1 fusion.154
  50.7 5.3 subtract_bitcast_fusion.2
  56.0 6.4 fusion.46
  62.4 7.2 subtract_bitcast_fusion.1
  72.0 6.6 fusion.44
  78.6 6.8 add_bitcast_fusion.1
  92.8 6.2 all-to-all-start.3
  99.2 24.7 %gather_fusion = s32[4096]{0:T(1024)S(1)} fusion(s32[16]{0:T(128)S(1)} %multiply_add_fusion, s32[4096]{0:T(1024)S(1)} %broadcast_clamp_fusion.1), kind=kCustom, calls=%fused_computation | custom fusion | bytes 49152 | tf_op jit(solution)/shard_map/gather | solution.py:112
  126.6 14.2 %gather_fusion.2 = f32[4096,128]{1,0:T(8,128)} fusion(f32[4096,128]{1,0:T(8,128)S(1)} %bitcast.336, s32[4096]{0:T(1024)S(1)} %broadcast_clamp_fusion), kind=kCustom, calls=%fused_computation.2 | custom fusion | bytes 4210688 | tf_op jit(solution)/shard_map/jit(_take)/gather | solution.py:113
  140.8 4.3 fusion.82
  159.1 4.2 copy.119
  163.3 4.8 reshape.318
  179.4 4.9 reshape.317
  192.2 12.1 %copy.121 = f32[16,16,2048]{1,0,2:T(8,128)} copy(f32[16,16,2048]{2,1,0:T(8,128)} %bitcast.360) | data formatting | bytes 4194304 | tf_op jit(solution)/shard_map/bmn,bf->mnf/dot_general | solution.py:70
  204.4 14.4 %reduce-scatter.2.cloned.1.call-done = f32[2,16,2048]{2,1,0:T(8,128)} async-done(((f32[2,16,8192]{2,1,0:T(8,128)}), f32[2,16,2048]{2,1,0:T(8,128)}) %reduce-scatter.2.cloned.1.call-update) | async-done | bytes 262160 | tf_op jit(solution)/shard_map/reduce_scatter | solution.py:131
  222.5 29.9 %convolution_bitcast_fusion.5 = f32[2,16,2048]{1,0,2:T(2,128)} fusion(f32[2,16,2048]{1,0,2:T(2,128)} %copy.120, f32[16,16,2048]{1,0,2:T(8,128)} %copy.121), kind=kOutput, calls=%fused_computation.121 | convolution fusion | flops 12582912 | bytes 2621440 | tf_op jit(solution)/shard_map/mnf,cnf->cmf/dot_general | solution.py:71
  252.3 3.9 copy.122
  257.2 29.9 %all-gather.2.cloned.1.call-done = f32[2,16,8192]{2,1,0:T(8,128)} async-done(((f32[2,16,2048]{2,1,0:T(8,128)}), f32[2,16,8192]{2,1,0:T(8,128)}) %all-gather.2.cloned.1.call-update) | async-done | bytes 1048592 | tf_op jit(solution)/shard_map/all_gather | solution.py:135
  287.1 3.9 fusion.87
  316.3 24.0 %scatter_custom_fusion.1 = f32[4096,128]{1,0:T(8,128)} fusion(s32[4096]{0:T(1024)S(1)} %bitcast.364, f32[4096,128]{1,0:T(8,128)} %fusion.438, f32[]{:T(128)} %constant.177.clone.1), kind=kCustom, calls=%fused_computation.129 | custom fusion | flops 524288 | bytes 2097664 | tf_op jit(solution)/shard_map/scatter-add | solution.py:147
  340.3 7.4 all-to-all-start.2
  347.7 11.5 %copy.134 = f32[32,128,512]{1,0,2:T(8,128)} copy(f32[32,128,512]{1,2,0:T(8,128)} %all-to-all-done.3) | data formatting | bytes 16777216 | tf_op jit(solution)/shard_map/all_to_all | solution.py:166
  359.3 9.4 %reshape.325 = f32[4096,2,256]{0,2,1:T(8,128)} reshape(f32[32,128,512]{1,0,2:T(8,128)} %copy.134) | data formatting | bytes 16777216 | tf_op jit(solution)/shard_map/reshape | solution.py:167
  368.6 7.8 slice_bitcast_fusion.1
  376.4 5.8 copy.137
  382.3 10.6 %fusion.38 = f32[256,64,64]{0,2,1:T(8,128)} fusion(f32[256,64,64]{0,2,1:T(8,128)} %bitcast.341), kind=kOutput, calls=%fused_computation.75 | convolution fusion | flops 805367808 | bytes 8388608 | tf_op jit(solution)/shard_map/ka,...ab->...kb/dot_general | solution.py:36
  392.9 7.2 fusion.36
  400.1 5.8 copy.135
  405.9 10.2 %fusion.56 = f32[256,64,64]{0,2,1:T(8,128)S(1)} fusion(f32[256,64,64]{0,2,1:T(8,128)} %fusion.38, f32[256,64,64]{0,2,1:T(8,128)} %bitcast.337), kind=kOutput, calls=%fused_computation.89 | convolution fusion | flops 806412288 | bytes 12582912 | tf_op jit(solution)/shard_map/ka,...ab->...kb/dot_general | solution.py:32
  416.2 9.4 %fusion.14 = (f32[256,64,64]{0,1,2:T(8,128)S(1)}, f32[256,64,64]{0,1,2:T(8,128)S(1)}) fusion(f32[256,64,64]{0,2,1:T(8,128)S(1)} %fusion.56, f32[64,64]{0,1:T(8,128)S(1)} %copy.142, f32[64,64]{0,1:T(8,128)S(1)} %copy.139, f32[256,64,64]{0,2,1:T(8,128)S(1)} %copy-done.14, f32[256,64,64]{0,2,1:T(8,128)S(1)} %bitcast.338), kind=kOutput, calls=%fused_computation.42 | convolution fusion | flops 812707840 | bytes 21004288 | tf_op jit(solution)/shard_map/ka,...ab->...kb/dot_general | solution.py:33
  425.7 6.7 fusion.28
  432.4 6.8 fusion.30
  439.2 7.9 fusion.8
  447.1 8.1 %fusion.9 = f32[256,64,64]{0,1,2:T(8,128)S(1)} fusion(f32[256,64,64]{0,2,1:T(8,128)S(1)} %fusion.30, f32[256,64,64]{0,1,2:T(8,128)S(1)} %get-tuple-element.9, f32[256]{0:T(256)S(1)} %fusion.258, f32[64,64]{0,1:T(8,128)S(1)} %copy.145), kind=kOutput, calls=%fused_computation.24 | convolution fusion | flops 813752320 | bytes 12600320 | tf_op jit(solution)/shard_map/qb,...kb->...qk/dot_general | solution.py:46
  455.2 4.4 fusion.165
  459.6 4.7 fusion.144
  464.4 4.4 convolution_subtract_fusion.1
  468.8 6.7 fusion.12
  475.4 6.9 fusion.22
  482.3 6.8 subtract_bitcast_fusion
  491.5 6.7 fusion.20
  498.2 7.0 add_bitcast_fusion
  507.6 4.3 maximum_bitcast_fusion.1
  511.9 9.0 %copy.155 = f32[32,128,2,256]{1,3,2,0:T(8,128)} copy(f32[32,128,2,256]{3,1,0,2:T(8,128)} %maximum_bitcast_fusion.1) | data formatting | bytes 16777216 | tf_op jit(solution)/shard_map/transpose | solution.py:180
  520.9 5.4 all-to-all-start.4
  530.2 6.7 scatter_fusion
  536.9 5.6 copy.124
  542.5 169.7 %all-to-all-done.4 = f32[32,128,512]{1,2,0:T(8,128)} async-done(((f32[32,128,512]{1,2,0:T(8,128)}), f32[32,128,512]{1,2,0:T(8,128)}, u32[]{:S(2)}, u32[]{:S(2)}) %all-to-all-start.4) | async-done | bytes 8388640 | tf_op jit(solution)/shard_map/all_to_all | solution.py:181
  712.1 7.8 fusion.435
  719.9 5.4 copy.162
  725.4 8.3 %fusion.159 = f32[128,128,64]{1,2,0:T(8,128)} fusion(f32[128,64,128]{2,1,0:T(8,128)} %copy.162), kind=kOutput, calls=%fused_computation.218 | convolution fusion | flops 805363712 | bytes 8388608 | tf_op jit(solution)/shard_map/ka,...ab->...kb/dot_general | solution.py:32
  733.7 5.5 fusion.139
  739.2 5.6 copy.163
  744.8 8.0 %convolution_subtract_fusion = f32[128,128,64]{1,2,0:T(8,128)S(1)} fusion(f32[128,128,64]{1,2,0:T(8,128)} %fusion.159, f32[128,64,128]{2,1,0:T(8,128)} %copy.163), kind=kOutput, calls=%fused_computation.92 | convolution fusion | flops 806412288 | bytes 12582912 | tf_op jit(solution)/shard_map/ka,...ab->...kb/dot_general | solution.py:36
  752.9 5.5 fusion.10
  758.4 6.9 fusion.16
  765.3 6.8 multiply_bitcast_fusion
  776.9 5.6 copy.161
  (128 shorter events, 93.0 us)
Async XLA Ops:
  6.5 183.4 %copy-start = (f32[32,16,16]{0,2,1:T(8,128)S(1)}, f32[32,16,16]{0,2,1:T(8,128)}, u32[]{:S(2)}) copy-start(f32[32,16,16]{0,2,1:T(8,128)} %param.17) | copy-start | bytes 98308
  10.3 18.4 %all-to-all-start = ((s32[8,1,4]{2,1,0:T(1,128)}), s32[8,1,4]{2,1,0:T(1,128)S(1)}, u32[]{:S(2)}, u32[]{:S(2)}) async-start(s32[8,1,4]{2,1,0:T(1,128)} %bitcast.3), calls=%async_computation | async-start | bytes 8192 | tf_op jit(solution)/shard_map/all_to_all | solution.py:103
  28.7 4.3 copy-start.19
  33.0 59.8 %all-to-all-start.1 = ((f32[8,4,128,128]{3,2,1,0:T(8,128)}), f32[8,4,128,128]{3,2,1,0:T(8,128)S(1)}, u32[]{:S(2)}, u32[]{:S(2)}) async-start(f32[8,4,128,128]{3,2,1,0:T(8,128)} %bitcast.361), calls=%async_computation.1 | async-start | bytes 4194304 | tf_op jit(solution)/shard_map/all_to_all | solution.py:108
  44.5 6.1 copy-start.9
  92.8 6.2 copy-start.18
  92.8 6.3 copy-start.22
  92.8 247.5 %all-to-all-start.3 = ((f32[32,128,512]{1,2,0:T(8,128)}), f32[32,128,512]{1,2,0:T(8,128)}, u32[]{:S(2)}, u32[]{:S(2)}) async-start(f32[32,128,512]{1,2,0:T(8,128)} %bitcast.343), calls=%async_computation.4 | async-start | bytes 16777216 | tf_op jit(solution)/shard_map/all_to_all | solution.py:166
  99.0 119.8 %reduce-scatter.2.cloned.1.call-start = ((), (), s32[]{:S(2)}) async-start(), calls=%async_computation.6 | async-start | bytes 1310720 | tf_op jit(solution)/shard_map/reduce_scatter | solution.py:131
  99.2 25.1 %copy-start.21 = (f32[64,32]{0,1:T(8,128)S(1)}, f32[64,32]{0,1:T(8,128)}, u32[]{:S(2)}) copy-start(f32[64,32]{0,1:T(8,128)} %param.15) | copy-start | bytes 24580
  126.6 14.2 %copy-start.16 = (f32[128,128]{1,0:T(8,128)S(1)}, f32[128,128]{1,0:T(8,128)}, u32[]{:S(2)}) copy-start(f32[128,128]{1,0:T(8,128)} %param.14) | copy-start | bytes 196612
  153.3 2.2 copy-start.2
  168.1 3.9 copy-start.3
  179.4 4.9 copy-start.4
  179.4 4.9 copy-start.17
  184.3 3.0 copy-start.10
  189.7 97.4 %all-gather.2.cloned.1.call-start = ((), (), s32[]{:S(2)}) async-start(), calls=%async_computation.7 | async-start | bytes 1310720 | tf_op jit(solution)/shard_map/all_gather | solution.py:135
  287.1 4.3 copy-start.11
  287.1 4.3 copy-start.15
  340.3 180.6 %all-to-all-start.2 = ((f32[8,4,128,128]{3,2,1,0:T(8,128)}), f32[8,4,128,128]{3,2,1,0:T(8,128)S(1)}, u32[]{:S(2)}, u32[]{:S(2)}) async-start(f32[8,4,128,128]{3,2,1,0:T(8,128)} %bitcast.362), calls=%async_computation.3 | async-start | bytes 4194304 | tf_op jit(solution)/shard_map/all_to_all | solution.py:149
  382.3 10.7 %copy-start.7 = (f32[256,4096]{0,1:T(8,128)S(1)}, f32[256,4096]{0,1:T(8,128)}, u32[]{:S(2)}) copy-start(f32[256,4096]{0,1:T(8,128)} %copy.137) | copy-start | bytes 12582916
  405.9 10.3 %copy-start.6 = (f32[256,4096]{0,1:T(8,128)S(1)}, f32[256,4096]{0,1:T(8,128)}, u32[]{:S(2)}) copy-start(f32[256,4096]{0,1:T(8,128)} %copy.135) | copy-start | bytes 12582916
  405.9 10.3 %copy-start.14 = (f32[256,64,64]{0,2,1:T(8,128)S(1)}, f32[256,64,64]{0,2,1:T(8,128)}, u32[]{:S(2)}) copy-start(f32[256,64,64]{0,2,1:T(8,128)} %fusion.36) | copy-start | bytes 12582916
  520.9 6.0 copy-start.20
  520.9 191.2 %all-to-all-start.4 = ((f32[32,128,512]{1,2,0:T(8,128)}), f32[32,128,512]{1,2,0:T(8,128)}, u32[]{:S(2)}, u32[]{:S(2)}) async-start(f32[32,128,512]{1,2,0:T(8,128)} %bitcast.344), calls=%async_computation.5 | async-start | bytes 16777216 | tf_op jit(solution)/shard_map/all_to_all | solution.py:181
  725.3 8.4 %copy-start.8 = (f32[128,64,128]{2,1,0:T(8,128)S(1)}, f32[128,64,128]{2,1,0:T(8,128)}, u32[]{:S(2)}) copy-start(f32[128,64,128]{2,1,0:T(8,128)} %copy.162) | copy-start | bytes 12582916
  744.8 8.1 %copy-start.5 = (f32[128,64,128]{2,1,0:T(8,128)S(1)}, f32[128,64,128]{2,1,0:T(8,128)}, u32[]{:S(2)}) copy-start(f32[128,64,128]{2,1,0:T(8,128)} %copy.163) | copy-start | bytes 12582916
  744.8 8.1 %copy-start.13 = (f32[128,128,64]{1,2,0:T(8,128)S(1)}, f32[128,128,64]{1,2,0:T(8,128)}, u32[]{:S(2)}) copy-start(f32[128,128,64]{1,2,0:T(8,128)} %fusion.139) | copy-start | bytes 12582916
  772.0 2.4 copy-start.12
  774.5 8.0 %copy-start.1 = (f32[32,16,16]{0,2,1:T(8,128)S(1)}, f32[32,16,16]{0,2,1:T(8,128)}, u32[]{:S(2)}) copy-start(f32[32,16,16]{0,2,1:T(8,128)} %param.17) | copy-start | bytes 98308
Sparse Core Ops, SparseCore 0:
  189.8 28.8 reduce-scatter.1
  256.4 30.6 all-gather.1
where the time goes:
time: 797 us; the launch traced here: 790 us
  matrix products  277 us (35%)
  waiting for transfers between devices  214 us (27%)
  local copies, waits for them, and re-layouts  207 us (26%)
  other arithmetic  45.4 us (6%)
  starting transfers between devices  32.3 us (4%)
  between operations  14.6 us (2%)
    all_to_all x1, waiting for transfers between devices, local(): lax.all_to_all(stacked, ('det', 'tm'), split_axis=0, concat_axis=0, tiled...  170 us
    dot_general x6, matrix products, transform_last(): jnp.einsum('qb,...kb->...qk', inner_real, turned_real, precision=precise)  34.9 us
    dot_general x6, matrix products, transform_last(): jnp.einsum('qb,...kb->...qk', inner_imag, turned_imag, precision=precise)  32.7 us
    dot_general x6, matrix products, transform_last(): jnp.einsum('ka,...ab->...kb', outer_real, shaped_real, precision=precise)  32.5 us
    dot_general x6, matrix products, transform_last(): jnp.einsum('ka,...ab->...kb', outer_imag, shaped_real, precision=precise)  30.1 us
    dot_general x1, matrix products, couple_modes(): jnp.einsum('mnf,cnf->cmf', kernel_freq, projection, precision=precise)  29.9 us
    all_gather x1, waiting for transfers between devices, local(): lax.all_gather(couple_modes(mode_share, mode_kernel, share_onehot), 'det'...  29.9 us
    dot_general x4, matrix products, transform_last(): jnp.einsum('qb,...kb->...qk', inner_imag, turned_real, precision=precise)  25.3 us
  transfers between devices with their start and end apart: 7, of which 3 were waited for; matrix products, arithmetic and copies ran while one was open for 57% of the time, Pallas kernels for 0%

commit v1 on v0

v1 whole, which is shorter than its diff:
```python
import functools
import math

import jax
import jax.numpy as jnp
import ml_dtypes
import numpy as np
from jax import lax
from jax.experimental import pallas as pl
from jax.experimental.pallas import tpu as pltpu
from jax.sharding import PartitionSpec as P

BAND_WIDTH = 128
LANES = 128
LIMIT = 50 * 1024 * 1024
F32 = jnp.float32
BF16 = jnp.bfloat16


def group_frequencies(length):
    half = LANES // 2
    outer = length // LANES
    steps = np.arange(LANES)
    freq = np.zeros((outer // 2, 2 * LANES), np.int64)
    for group in range(1, outer // 2):
        freq[group] = np.concatenate([group + outer * steps] * 2)
    low = outer * np.concatenate([np.arange(half + 1), np.arange(1, half)])
    middle = outer // 2 + outer * np.concatenate([np.arange(half)] * 2)
    freq[0] = np.concatenate([low, middle])
    return freq


def group_tables(length):
    half = LANES // 2
    freq = group_frequencies(length)
    groups = freq.shape[0]
    steps = np.arange(LANES)
    forward = np.zeros((groups, 2 * LANES, 2 * LANES))
    weight = np.ones((groups, 2 * LANES))
    angle = 2.0 * math.pi / length
    for group in range(groups):
        turn = (steps[:, None] * freq[group][None, :] % length) * angle
        cosine, sine = np.cos(turn), np.sin(turn)
        if group > 0:
            forward[group, :LANES, :LANES] = cosine[:, :LANES]
            forward[group, LANES:, :LANES] = sine[:, :LANES]
            forward[group, :LANES, LANES:] = -sine[:, LANES:]
            forward[group, LANES:, LANES:] = cosine[:, LANES:]
        else:
            forward[0, :LANES, : half + 1] = cosine[:, : half + 1]
            forward[0, :LANES, half + 1 : LANES] = -sine[:, half + 1 : LANES]
            forward[0, LANES:, LANES : LANES + half] = cosine[:, LANES : LANES + half]
            forward[0, LANES:, LANES + half :] = -sine[:, LANES + half :]
            weight[0, :] = 2.0
            weight[0, 0] = 1.0
            weight[0, half] = 1.0
    backward = (forward * weight[:, None, :] / length).transpose(0, 2, 1)
    return forward, backward


def halves(table):
    high = table.astype(np.float32).astype(ml_dtypes.bfloat16)
    low = (table - high.astype(np.float64)).astype(ml_dtypes.bfloat16)
    return high, low


def split(value):
    high = value.astype(BF16)
    return high, (value - high.astype(F32)).astype(BF16)


def multiply(left, right, dims=(((1,), (0,)), ((), ()))):
    dot = functools.partial(lax.dot_general, dimension_numbers=dims, preferred_element_type=F32)
    return dot(left[0], right[0]) + (dot(left[1], right[0]) + dot(left[0], right[1]))


def forward_stage(load, start, step, count):
    if count == 2:
        first, second = load(start), load(start + step)
        return [(first + second, None), (first - second, None)]
    even = forward_stage(load, start, 2 * step, count // 2)
    odd = forward_stage(load, start + step, 2 * step, count // 2)
    out = [None] * (count // 2 + 1)
    out[0] = (even[0][0] + odd[0][0], None)
    out[count // 2] = (even[0][0] - odd[0][0], None)
    out[count // 4] = (even[count // 4][0], -odd[count // 4][0])
    for k in range(1, count // 4):
        cosine, sine = math.cos(2 * math.pi * k / count), math.sin(2 * math.pi * k / count)
        odd_re, odd_im = odd[k]
        turn_re = cosine * odd_re + sine * odd_im
        turn_im = cosine * odd_im - sine * odd_re
        out[k] = (even[k][0] + turn_re, even[k][1] + turn_im)
        out[count // 2 - k] = (even[k][0] - turn_re, turn_im - even[k][1])
    return out


def backward_stage(spec, store, start, step):
    count = 2 * (len(spec) - 1)
    if count == 2:
        store(start, spec[0][0] + spec[1][0])
        store(start + step, spec[0][0] - spec[1][0])
        return
    even, odd = [None] * (count // 4 + 1), [None] * (count // 4 + 1)
    even[0] = (spec[0][0] + spec[count // 2][0], None)
    odd[0] = (spec[0][0] - spec[count // 2][0], None)
    middle = spec[count // 4]
    even[count // 4] = (2.0 * middle[0], None)
    odd[count // 4] = (-2.0 * middle[1], None)
    for k in range(1, count // 4):
        cosine, sine = math.cos(2 * math.pi * k / count), math.sin(2 * math.pi * k / count)
        (a_re, a_im), (b_re, b_im) = spec[k], spec[count // 2 - k]
        even[k] = (a_re + b_re, a_im - b_im)
        diff_re, diff_im = a_re - b_re, a_im + b_im
        odd[k] = (diff_re * cosine - diff_im * sine, diff_re * sine + diff_im * cosine)
    backward_stage(even, store, start, 2 * step)
    backward_stage(odd, store, start + step, 2 * step)


def rows_forward(load_tile, held, rows, outer):
    def body(index, carry):
        at = pl.ds(pl.multiple_of(index * 8, 8), 8)
        spec = forward_stage(lambda tile: load_tile(tile, at), 0, 1, outer)
        held[0, at, :LANES] = spec[0][0]
        held[0, at, LANES:] = spec[outer // 2][0]
        for k in range(1, outer // 2):
            held[k, at, :LANES] = spec[k][0]
            held[k, at, LANES:] = spec[k][1]
        return carry

    lax.fori_loop(0, rows // 8, body, 0)


def rows_backward(store_tile, held, rows, outer):
    def body(index, carry):
        at = pl.ds(pl.multiple_of(index * 8, 8), 8)
        spec = [(held[0, at, :LANES], None)]
        for k in range(1, outer // 2):
            spec.append((held[k, at, :LANES], held[k, at, LANES:]))
        spec.append((held[0, at, LANES:], None))
        backward_stage(spec, lambda tile, value: store_tile(tile, at, value), 0, 1)
        return carry

    lax.fori_loop(0, rows // 8, body, 0)


def pick_kernel(ids, sky, out):
    slots, last = out.shape[0], sky.shape[1] // LANES - 1

    def body(slot, carry):
        at = pl.multiple_of(jnp.minimum(ids[slot], last) * LANES, LANES)
        out[slot] = sky[:, pl.ds(at, LANES)]
        return carry

    lax.fori_loop(0, slots, body, 0)


def sky_forward_kernel(sky, high, low, out, held):
    rows, width = sky.shape
    group = pl.program_id(0)

    @pl.when(group == 0)
    def _():
        def load(tile, at):
            return sky[at, tile * LANES : (tile + 1) * LANES]

        rows_forward(load, held, rows, width // LANES)

    out[0] = multiply(split(held[group]), (high[0], low[0]))


def column_kernel(cols, row_sq, col_sq, f_high, f_low, b_high, b_low, out, held, *, knee_sq):
    length, width = cols.shape
    outer = length // LANES
    group = pl.program_id(0)
    chunks = [(at, min(LANES, width)) for at in range(0, width, LANES)]

    @pl.when(group == 0)
    def _():
        def body(index, carry):
            first = pl.multiple_of(index * 8, 8)
            near, far = pl.ds(first, 8), pl.ds(pl.multiple_of(first + LANES, 8), 8)
            for start, size in chunks:
                lanes = slice(start, start + size)

                def load(tile):
                    return cols[pl.ds(pl.multiple_of(tile * LANES + first, 8), 8), lanes]

                spec = forward_stage(load, 0, 1, outer)
                held[0, near, lanes] = spec[0][0]
                held[0, far, lanes] = spec[outer // 2][0]
                for k in range(1, outer // 2):
                    held[k, near, lanes] = spec[k][0]
                    held[k, far, lanes] = spec[k][1]
            return carry

        lax.fori_loop(0, LANES // 8, body, 0)

    spectrum = multiply((f_high[0], f_low[0]), split(held[group]))
    radial_sq = row_sq[0] + col_sq[...]
    gain = 1.0 + radial_sq * 20.0 + 0.25 * lax.rsqrt(radial_sq + knee_sq)
    held[group] = multiply((b_high[0], b_low[0]), split(spectrum * gain))

    @pl.when(group == pl.num_programs(0) - 1)
    def _():
        def body(index, carry):
            first = pl.multiple_of(index * 8, 8)
            near, far = pl.ds(first, 8), pl.ds(pl.multiple_of(first + LANES, 8), 8)
            for start, size in chunks:
                lanes = slice(start, start + size)
                spec = [(held[0, near, lanes], None)]
                for k in range(1, outer // 2):
                    spec.append((held[k, near, lanes], held[k, far, lanes]))
                spec.append((held[0, far, lanes], None))

                def store(tile, value):
                    out[pl.ds(pl.multiple_of(tile * LANES + first, 8), 8), lanes] = value

                backward_stage(spec, store, 0, 1)
            return carry

        lax.fori_loop(0, LANES // 8, body, 0)


def finish_kernel(ids, spectrum, high, low, delivered, out, held):
    rows, width = out.shape
    group = pl.program_id(0)
    held[group] = multiply(split(spectrum[0]), (high[0], low[0]))

    @pl.when(group == pl.num_programs(0) - 1)
    def _():
        def store(tile, at, value):
            out[at, tile * LANES : (tile + 1) * LANES] = -value

        rows_backward(store, held, rows, width // LANES)

        def body(slot, carry):
            block = ids[slot]

            @pl.when(block < width // LANES)
            def _():
                at = pl.ds(pl.multiple_of(block * LANES, LANES), LANES)
                out[:, at] = out[:, at] + delivered[slot]

            return carry

        lax.fori_loop(0, delivered.shape[0], body, 0)


def data_forward_kernel(
    pointing, slots, arrived, data, beam, white, loading, high, low, spec_out, proj_out, held, listed, tiles
):
    dets, width = data.shape
    outer = width // LANES
    wanted, block_rows = slots.shape[0], arrived.shape[1]
    group = pl.program_id(0)

    @pl.when(group == 0)
    def _():
        def place(entry, carry):
            at = pl.ds(pl.multiple_of(entry * block_rows, 8), block_rows)
            listed[at, :] = arrived[slots[entry]]
            return carry

        lax.fori_loop(0, wanted, place, 0)
        response = split(beam[...])

        def fetch(tile, carry):
            for det in range(dets):
                tiles[tile, det : det + 1, :] = listed[pl.ds(pointing[det, tile], 1), :]
            return carry

        lax.fori_loop(0, outer, fetch, 0)

        for tile in range(outer):
            signal = multiply(split(tiles[tile]), response, (((1,), (1,)), ((), ())))
            tiles[tile] = data[:, tile * LANES : (tile + 1) * LANES] - signal

        rows_forward(lambda tile, at: tiles[tile, at, :], held, dets, outer)

    spec = multiply(split(held[group]), (high[0], low[0]))
    spec_out[0] = spec
    proj_out[0] = multiply(split(loading[...]), split(white[0] * spec), (((0,), (0,)), ((), ())))


def data_backward_kernel(
    pointing, slots, spec, proj, coupling, beam, white, loading, high, low, out, held, tiles, first, second, third, fourth
):
    dets = spec.shape[1]
    modes = proj.shape[1]
    outer = tiles.shape[0]
    wanted, block_rows = slots.shape[0], out.shape[1]
    group = pl.program_id(0)
    coupled = coupling[0, 0] * proj[0, 0:1, :]
    for mode in range(1, modes):
        coupled = coupled + coupling[0, mode] * proj[0, mode : mode + 1, :]
    common = multiply(split(loading[...]), split(coupled))
    filtered = white[0] * (spec[0] - common)
    held[group] = multiply(split(filtered), (high[0], low[0]))

    @pl.when(group == pl.num_programs(0) - 1)
    def _():
        def store(tile, at, value):
            tiles[tile, at, :] = value

        rows_backward(store, held, dets, outer)
        sums = (first, second, third, fourth)
        for total in sums:
            total[...] = jnp.zeros_like(total)
        out[...] = jnp.zeros_like(out)
        response = split(beam[...])
        for tile in range(outer):
            tiles[tile] = multiply(split(tiles[tile]), response)

        def add(tile, carry):
            for det in range(dets):
                total = sums[det % 4]
                at = pl.ds(pointing[det, tile], 1)
                total[at, :] = total[at, :] + tiles[tile, det : det + 1, :]
            return carry

        lax.fori_loop(0, outer, add, 0)

        def place(entry, carry):
            at = pl.ds(pl.multiple_of(entry * block_rows, 8), block_rows)
            out[slots[entry]] = (first[at, :] + second[at, :]) + (third[at, :] + fourth[at, :])
            return carry

        lax.fori_loop(0, wanted, place, 0)


SCALARS = pl.BlockSpec(memory_space=pltpu.SMEM)


def whole(array):
    return pl.BlockSpec(array.shape, lambda g, n=len(array.shape): (0,) * n)


def sliced(array):
    return pl.BlockSpec((1,) + array.shape[1:], lambda g, n=len(array.shape): (g,) + (0,) * (n - 1))


def first_or_rest(array):
    return pl.BlockSpec(
        (1,) + array.shape[1:], lambda g, n=len(array.shape): (jnp.minimum(g, 1),) + (0,) * (n - 1)
    )


PARAMS = pltpu.CompilerParams(vmem_limit_bytes=LIMIT)


def struct(*shape):
    return jax.ShapeDtypeStruct(shape, F32)


def local(
    detector_data,
    sky_map,
    pointing,
    request_owner,
    request_block,
    beam_kernel,
    inv_white,
    mode_loading,
    mode_kernel,
):
    dets, samples = detector_data.shape
    rows_here, map_cols = sky_map.shape
    owners = lax.axis_size("tm")
    devices = lax.axis_size("det") * owners
    tile = beam_kernel.shape[0]
    blocks_here = map_cols // tile
    wanted = request_owner.shape[0]
    capacity = max(2, 2 * wanted // owners)
    slots = owners * capacity
    modes = mode_loading.shape[1]
    bands = inv_white.shape[1]
    per_device = map_cols // devices
    total_rows = rows_here * devices
    wide = 2 * LANES

    row_forward, row_backward = [halves(t) for t in group_tables(map_cols)]
    row_forward = [jnp.asarray(t) for t in row_forward]
    row_backward = [jnp.asarray(t) for t in row_backward]
    if samples == map_cols:
        time_forward, time_backward = row_forward, row_backward
    else:
        time_forward, time_backward = [[jnp.asarray(h) for h in halves(t)] for t in group_tables(samples)]
    col_f, col_b = group_tables(total_rows)
    col_forward = [jnp.asarray(t) for t in halves(col_f.transpose(0, 2, 1))]
    col_backward = [jnp.asarray(t) for t in halves(col_b.transpose(0, 2, 1))]
    groups = map_cols // LANES // 2
    time_groups = samples // LANES // 2
    col_groups = total_rows // LANES // 2

    target = request_owner[:, 0]
    entry = jnp.arange(wanted, dtype=jnp.int32)
    earlier = (target[:, None] == target[None, :]) & (entry[None, :] < entry[:, None])
    slot_index = target * capacity + jnp.sum(earlier.astype(jnp.int32), axis=1)
    named = slot_index[None, :] == jnp.arange(slots, dtype=jnp.int32)[:, None]
    send_ids = blocks_here + jnp.sum(jnp.where(named, request_block[None, :] - blocks_here, 0), axis=1)
    asked_ids = lax.all_to_all(
        send_ids.reshape(owners, capacity), "tm", split_axis=0, concat_axis=0, tiled=True
    ).reshape(-1)

    outgoing = pl.pallas_call(
        pick_kernel,
        in_specs=[SCALARS, pl.BlockSpec(memory_space=pltpu.VMEM)],
        out_specs=pl.BlockSpec(memory_space=pltpu.VMEM),
        out_shape=struct(slots, rows_here, tile),
        compiler_params=PARAMS,
        name="pick_blocks",
    )(asked_ids, sky_map)
    arrived = lax.all_to_all(
        outgoing.reshape(owners, capacity, rows_here, tile), "tm", split_axis=0, concat_axis=0, tiled=True
    ).reshape(slots, rows_here, tile)

    packed = pl.pallas_call(
        sky_forward_kernel,
        grid=(groups,),
        in_specs=[whole(sky_map), sliced(row_forward[0]), sliced(row_forward[1])],
        out_specs=pl.BlockSpec((1, rows_here, wide), lambda g: (g, 0, 0)),
        out_shape=struct(groups, rows_here, wide),
        scratch_shapes=[pltpu.VMEM((groups, rows_here, wide), F32)],
        compiler_params=PARAMS,
        name="sky_forward",
    )(sky_map, *row_forward)
    parts = wide // per_device
    if parts > 1:
        packed = packed.reshape(groups, rows_here, parts, per_device).transpose(0, 2, 1, 3)
        packed = packed.reshape(devices, rows_here, per_device)
    columns = lax.all_to_all(packed, ("det", "tm"), split_axis=0, concat_axis=0, tiled=True)
    columns = columns.reshape(total_rows, per_device)

    freq = group_frequencies(samples)[:2]
    band = np.minimum(np.minimum(freq, samples - freq) // BAND_WIDTH, bands - 1)
    onehot = jnp.asarray((np.arange(bands)[:, None, None] == band[None]).astype(np.float32))
    precise = lax.Precision.HIGHEST
    white = jnp.einsum("jb,bgf->gjf", inv_white, onehot, precision=precise)
    coupling = jnp.einsum("bmn,bgf->gnmf", mode_kernel, onehot, precision=precise)
    spec, proj = pl.pallas_call(
        data_forward_kernel,
        grid=(time_groups,),
        in_specs=[
            SCALARS,
            SCALARS,
            whole(arrived),
            whole(detector_data),
            whole(beam_kernel),
            first_or_rest(white),
            whole(mode_loading),
            sliced(time_forward[0]),
            sliced(time_forward[1]),
        ],
        out_specs=[
            pl.BlockSpec((1, dets, wide), lambda g: (g, 0, 0)),
            pl.BlockSpec((1, modes, wide), lambda g: (g, 0, 0)),
        ],
        out_shape=[struct(time_groups, dets, wide), struct(time_groups, modes, wide)],
        scratch_shapes=[
            pltpu.VMEM((time_groups, dets, wide), F32),
            pltpu.VMEM((wanted * rows_here, tile), F32),
            pltpu.VMEM((samples // tile, dets, tile), F32),
        ],
        compiler_params=PARAMS,
        name="data_forward",
    )(pointing, slot_index, arrived, detector_data, beam_kernel, white, mode_loading, *time_forward)
    proj = lax.psum(proj, "det")

    returned = pl.pallas_call(
        data_backward_kernel,
        grid=(time_groups,),
        in_specs=[
            SCALARS,
            SCALARS,
            sliced(spec),
            sliced(proj),
            first_or_rest(coupling),
            whole(beam_kernel),
            first_or_rest(white),
            whole(mode_loading),
            sliced(time_backward[0]),
            sliced(time_backward[1]),
        ],
        out_specs=pl.BlockSpec((slots, rows_here, tile), lambda g: (0, 0, 0)),
        out_shape=struct(slots, rows_here, tile),
        scratch_shapes=[
            pltpu.VMEM((time_groups, dets, wide), F32),
            pltpu.VMEM((samples // tile, dets, tile), F32),
        ]
        + [pltpu.VMEM((wanted * rows_here, tile), F32)] * 4,
        compiler_params=PARAMS,
        name="data_backward",
    )(pointing, slot_index, spec, proj, coupling, beam_kernel, white, mode_loading, *time_backward)
    delivered = lax.all_to_all(
        returned.reshape(owners, capacity, rows_here, tile), "tm", split_axis=0, concat_axis=0, tiled=True
    ).reshape(slots, rows_here, tile)

    rank = lax.axis_index("det") * owners + lax.axis_index("tm")
    col_freq = group_frequencies(map_cols).reshape(-1)
    col_sq = (np.minimum(col_freq, map_cols - col_freq) / map_cols) ** 2
    col_sq = lax.dynamic_slice_in_dim(
        jnp.asarray(col_sq.astype(np.float32).reshape(devices, per_device)), rank, 1, 0
    )
    row_freq = group_frequencies(total_rows)
    row_sq = ((np.minimum(row_freq, total_rows - row_freq) / total_rows) ** 2).astype(np.float32)
    row_sq = jnp.asarray(row_sq[:, :, None])
    knee_sq = 1.0 / (2.0 * math.pi * total_rows / 64.0) ** 2
    backed = pl.pallas_call(
        functools.partial(column_kernel, knee_sq=knee_sq),
        grid=(col_groups,),
        in_specs=[whole(columns), sliced(row_sq), whole(col_sq)]
        + [sliced(t) for t in col_forward + col_backward],
        out_specs=pl.BlockSpec((total_rows, per_device), lambda g: (0, 0)),
        out_shape=struct(total_rows, per_device),
        scratch_shapes=[pltpu.VMEM((col_groups, wide, per_device), F32)],
        compiler_params=PARAMS,
        name="sky_columns",
    )(columns, row_sq, col_sq, *col_forward, *col_backward)
    spectrum = lax.all_to_all(
        backed.reshape(devices, rows_here, per_device),
        ("det", "tm"),
        split_axis=0,
        concat_axis=0,
        tiled=True,
    )
    if parts > 1:
        spectrum = spectrum.reshape(groups, parts, rows_here, per_device).transpose(0, 2, 1, 3)
        spectrum = spectrum.reshape(groups, rows_here, wide)

    return pl.pallas_call(
        finish_kernel,
        grid=(groups,),
        in_specs=[
            SCALARS,
            sliced(spectrum),
            sliced(row_backward[0]),
            sliced(row_backward[1]),
            whole(delivered),
        ],
        out_specs=pl.BlockSpec((rows_here, map_cols), lambda g: (0, 0)),
        out_shape=struct(rows_here, map_cols),
        scratch_shapes=[pltpu.VMEM((groups, rows_here, wide), F32)],
        compiler_params=PARAMS,
        name="sky_finish",
    )(asked_ids, spectrum, *row_backward, delivered)


def solution(mesh):
    return jax.shard_map(
        local,
        mesh=mesh,
        in_specs=(
            P("det", "tm"),
            P(("det", "tm"), None),
            P("det", "tm"),
            P(("det", "tm"), None),
            P(("det", "tm")),
            P(),
            P("det", None),
            P("det", None),
            P(),
        ),
        out_specs=P(("det", "tm"), None),
        check_vma=False,
    )
```

time: 797 us -> 382 us (0.48)
  matrix products: 277 us -> 0.86 us
  local copies, waits for them, and re-layouts: 207 us -> 6.77 us
  Pallas kernels: 0 us -> 143 us
  waiting for transfers between devices: 214 us -> 85 us
  blocking collectives: 0 us -> 112 us
  other arithmetic: 45.4 us -> 2.35 us
  starting transfers between devices: 32.3 us -> 15.9 us
    dot_general x48 -> x2, matrix products: 274 us -> 0.86 us  [the longest x1 0.56 us: local(): jnp.einsum('bmn,bgf->gnmf', mode_kernel, onehot, precision=precise)]
    pallas_call x0 -> x6, Pallas kernels: none -> 143 us  [the longest x1 34.4 us: local(): pl.pallas_call(data_forward_kernel, grid=(time_groups,), in_specs=[SCALAR...]
    all_to_all x4 -> x2, waiting for transfers between devices: 170 us -> 45.4 us  [the longest x1 23 us: local(): lax.all_to_all(returned.reshape(owners, capacity, rows_here, tile), 'tm',...]
    all_to_all x0 -> x2, blocking collectives: none -> 112 us  [the longest x1 98.5 us: local(): lax.all_to_all(backed.reshape(devices, rows_here, per_device), ('det', 't...]
    gather x3 -> x0, local copies, waits for them, and re-layouts: 43.1 us -> none  [the longest x1 24.7 us: local(): row_index = (slot_index[list_slot] * rows_here + block_row).reshape(-1)]
    transpose x7 -> x0, local copies, waits for them, and re-layouts: 41.8 us -> none  [the longest x2 13.6 us: local(): col_real = columns[:, 0, :].T]
    psum x0 -> x1, waiting for transfers between devices: none -> 39.5 us  [local(): proj = lax.psum(proj, 'det')]
    reshape x9 -> x1, local copies, waits for them, and re-layouts: 32 us -> 0.08 us  [local(): asked_ids = lax.all_to_all(send_ids.reshape(owners, capacity), 'tm', spli...]
  transfers between devices with their start and end apart: 7 -> 4, of which waited for: 3 -> 3; matrix products, arithmetic and copies ran while one was open for 57% -> 0% of each run, Pallas kernels for 0% -> 30%
where the time goes in v1:
time: 382 us; the launch traced here: 379 us
  Pallas kernels  143 us (37%)
  blocking collectives  112 us (29%)
  waiting for transfers between devices  85 us (22%)
  starting transfers between devices  15.9 us (4%)
  between operations  13.5 us (4%)
  local copies, waits for them, and re-layouts  6.77 us (2%)
    all_to_all x1, blocking collectives, local(): lax.all_to_all(backed.reshape(devices, rows_here, per_device), ('det', 't...  98.5 us
    psum x1, waiting for transfers between devices, local(): proj = lax.psum(proj, 'det')  39.5 us
    pallas_call x1, Pallas kernels, local(): pl.pallas_call(data_forward_kernel, grid=(time_groups,), in_specs=[SCALAR...  34.4 us
    pallas_call x1, Pallas kernels, local(): pl.pallas_call(data_backward_kernel, grid=(time_groups,), in_specs=[SCALA...  33.4 us
    pallas_call x1, Pallas kernels, local(): pl.pallas_call(finish_kernel, grid=(groups,), in_specs=[SCALARS, sliced(s...  25 us
    pallas_call x1, Pallas kernels, local(): pl.pallas_call(sky_forward_kernel, grid=(groups,), in_specs=[whole(sky_ma...  24.5 us
    all_to_all x1, waiting for transfers between devices, local(): lax.all_to_all(returned.reshape(owners, capacity, rows_here, tile), 'tm',...  23 us
    all_to_all x1, waiting for transfers between devices, local(): lax.all_to_all(outgoing.reshape(owners, capacity, rows_here, tile), 'tm',...  22.4 us
  transfers between devices with their start and end apart: 4, of which 3 were waited for; matrix products, arithmetic and copies ran while one was open for 0% of the time, Pallas kernels for 30%

profile of v1, /device:TPU:0, one launch (start us, length us, event | category | flops | bytes accessed | tf_op | source)
XLA Modules:
  0.0 379.3 jit_solution(10556490097697795312)
XLA Ops:
  6.5 0.0 copy-start
  6.5 0.9 convert_reduce_fusion
  7.4 0.7 multiply_add_fusion
  8.1 0.1 select_reduce_fusion
  8.2 0.1 add.33
  8.3 13.5 %all_to_all.26 = s32[8,1,4]{2,1,0:T(1,128)S(1)} all-to-all(s32[8,1,4]{2,1,0:T(1,128)S(1)} %bitcast.27), channel_id=1, replica_groups=mesh['det'=4,'tm'=8] {'tm'}, dimensions={0} | all-to-all | bytes 256 | tf_op jit(solution)/shard_map/all_to_all | solution.py:401
  21.8 0.5 broadcast.30
  22.3 0.7 reduce.3
  23.0 0.1 reshape.49.ids
  23.1 4.0 %pick_blocks.1 = f32[32,128,128]{2,1,0:T(8,128)} custom-call(s32[32]{0:T(128)S(1)} %reshape.49.ids, f32[128,8192]{1,0:T(8,128)} %sky.3), custom_call_target="tpu_custom_call" | custom-call | tf_op jit(solution)/shard_map/pick_blocks/pallas_call | solution.py:405
  27.1 3.6 all-to-all-start.3
  30.7 24.5 %sky_forward.1 = f32[32,128,256]{2,1,0:T(8,128)} custom-call(f32[128,8192]{1,0:T(8,128)} %sky.3, bf16[32,256,256]{2,1,0:T(8,128)(2,1)} %constant.43.clone.high, bf16[32,256,256]{2,1,0:T(8,128)(2,1)} %constant.44.clone.low), custom_call_target="tpu_custom_call" | custom-call | tf_op jit(solution)/shard_map/sky_forward/pallas_call | solution.py:417
  55.3 0.0 copy-start.11
  55.3 0.0 copy-start.9
  55.3 0.0 copy-start.5
  55.3 0.0 copy-start.6
  55.3 22.4 %all-to-all-done.3 = f32[8,4,128,128]{3,2,1,0:T(8,128)S(1)} async-done(((f32[8,4,128,128]{3,2,1,0:T(8,128)}), f32[8,4,128,128]{3,2,1,0:T(8,128)S(1)}, u32[]{:S(2)}, u32[]{:S(2)}) %all-to-all-start.3) | async-done | bytes 2097184 | tf_op jit(solution)/shard_map/all_to_all | solution.py:413
  77.7 0.0 copy-start.7
  77.7 1.3 copy-done.7
  79.0 3.8 all-to-all-start.1
  82.8 0.0 all-reduce.2.cloned.1.call-start
  82.9 0.0 copy-done.11
  82.9 0.1 copy.32.loading
  83.0 0.0 copy-done
  83.0 0.0 copy-done.9
  83.0 0.3 convolution_bitcast_fusion.1.white
  83.3 0.0 copy-done.5
  83.3 0.0 copy-done.6
  83.3 0.0 copy-start.8
  83.3 0.0 copy-start.10
  83.4 34.4 %data_forward.1 = (f32[32,64,256]{2,1,0:T(8,128)S(1)}, f32[32,16,256]{2,1,0:T(8,128)}) custom-call(s32[64,64]{1,0:T(8,128)S(1)} %copy-done.6, s32[16]{0:T(128)S(1)} %get-tuple-element.9.slots, f32[32,128,128]{2,1,0:T(8,128)} %bitcast.26, f32[64,8192]{1,0:T(8,128)} %data.1, f32[128,128]{1,0:T(8,128)S(1)} %copy-done.5, ...), custom_call_target="tpu_custom_call" | custom-call | tf_op jit(solution)/shard_map/data_forward/pallas_call | solution.py:440
  117.7 0.0 copy-start.3
  117.7 1.3 copy-done.3
  119.1 0.0 all-reduce.2.cloned.1.call-update
  119.1 0.0 copy-done.8
  119.1 0.0 copy-done.10
  119.1 0.6 convolution_bitcast_fusion.coupling
  119.7 39.5 %all-reduce.2.cloned.1.call-done.proj = f32[32,16,256]{2,1,0:T(8,128)} async-done(((f32[32,16,256]{2,1,0:T(8,128)}), f32[32,16,256]{2,1,0:T(8,128)}) %all-reduce.2.cloned.1.call-update) | async-done | bytes 524304 | tf_op jit(solution)/shard_map/psum | solution.py:467
  159.2 0.0 copy-start.4
  159.2 1.0 copy-done.4
  160.2 33.4 %data_backward.1 = f32[32,128,128]{2,1,0:T(8,128)} custom-call(s32[64,64]{1,0:T(8,128)S(1)} %copy-done.6, s32[16]{0:T(128)S(1)} %get-tuple-element.9.slots, f32[32,64,256]{2,1,0:T(8,128)} %copy-done.3, f32[32,16,256]{2,1,0:T(8,128)S(1)} %copy-done.4, f32[2,16,16,256]{3,2,1,0:T(8,128)S(1)} %convolution_bitcast_fusion.coupling, f32[128,128]{1,0:T(8,128)S(1)} %copy-done.5, ...), custom_call_target="tpu_custom_call" | custom-call | tf_op jit(solution)/shard_map/data_backward/pallas_call | solution.py:469
  193.7 0.0 all-to-all-done.1
  193.7 8.5 %all-to-all-start.4 = ((f32[8,4,128,128]{3,2,1,0:T(8,128)}), f32[8,4,128,128]{3,2,1,0:T(8,128)S(1)}, u32[]{:S(2)}, u32[]{:S(2)}) async-start(f32[8,4,128,128]{3,2,1,0:T(8,128)} %bitcast.12), calls=%async_computation.4 | async-start | bytes 4194304 | tf_op jit(solution)/shard_map/all_to_all | solution.py:494
  202.2 0.7 constant_dynamic-slice_fusion.col_sq
  202.9 0.0 copy-start.2
  202.9 1.6 copy-done.2
  204.5 21.5 %sky_columns.1 = f32[4096,256]{1,0:T(8,128)} custom-call(f32[4096,256]{1,0:T(8,128)} %bitcast.2.cols, f32[16,256,1]{2,1,0:T(8,128)S(1)} %copy-done.2, f32[1,256]{1,0:T(1,128)S(1)} %constant_dynamic-slice_fusion.col_sq, bf16[16,256,256]{2,1,0:T(8,128)(2,1)} %constant.47.clone.f_high, bf16[16,256,256]{2,1,0:T(8,128)(2,1)} %constant.48.clone.f_low, ...), custom_call_target="tpu_custom_call" | custom-call | tf_op jit(solution)/shard_map/sky_columns/pallas_call | solution.py:508
  225.9 23.0 %all-to-all-done.4 = f32[8,4,128,128]{3,2,1,0:T(8,128)S(1)} async-done(((f32[8,4,128,128]{3,2,1,0:T(8,128)}), f32[8,4,128,128]{3,2,1,0:T(8,128)S(1)}, u32[]{:S(2)}, u32[]{:S(2)}) %all-to-all-start.4) | async-done | bytes 2097184 | tf_op jit(solution)/shard_map/all_to_all | solution.py:494
  248.9 98.5 %all_to_all.27.spectrum = f32[32,128,256]{2,1,0:T(8,128)} all-to-all(f32[32,128,256]{2,1,0:T(8,128)} %bitcast.25), channel_id=1, replica_groups=mesh['det'=4,'tm'=8] {'det','tm'}, dimensions={0} | all-to-all | bytes 8388608 | tf_op jit(solution)/shard_map/all_to_all | solution.py:519
  347.4 0.0 copy-start.1
  347.4 25.0 %sky_finish.1 = f32[128,8192]{1,0:T(8,128)} custom-call(s32[32]{0:T(128)S(1)} %reshape.49.ids, f32[32,128,256]{2,1,0:T(8,128)} %all_to_all.27.spectrum, bf16[32,256,256]{2,1,0:T(8,128)(2,1)} %constant.45.clone.high, bf16[32,256,256]{2,1,0:T(8,128)(2,1)} %constant.46.clone.low, f32[32,128,128]{2,1,0:T(8,128)S(1)} %bitcast.24), custom_call_target="tpu_custom_call" | custom-call | tf_op jit(solution)/shard_map/sky_finish/pallas_call | solution.py:530
  372.5 0.0 copy-done.1
  (1 shorter events, 0.0 us)
Async XLA Ops:
  6.5 76.5 %copy-start = (f32[64,32]{0,1:T(8,128)S(1)}, f32[64,32]{0,1:T(8,128)}, u32[]{:S(2)}) copy-start(f32[64,32]{0,1:T(8,128)} %param.26) | copy-start | bytes 24580
  27.1 50.6 %all-to-all-start.3 = ((f32[8,4,128,128]{3,2,1,0:T(8,128)}), f32[8,4,128,128]{3,2,1,0:T(8,128)S(1)}, u32[]{:S(2)}, u32[]{:S(2)}) async-start(f32[8,4,128,128]{3,2,1,0:T(8,128)} %bitcast.4), calls=%async_computation.3 | async-start | bytes 4194304 | tf_op jit(solution)/shard_map/all_to_all | solution.py:413
  55.3 27.6 %copy-start.11 = (f32[64,16]{0,1:T(8,128)S(1)}, f32[64,16]{0,1:T(8,128)}, u32[]{:S(2)}) copy-start(f32[64,16]{0,1:T(8,128)} %param.27) | copy-start | bytes 12292
  55.3 27.7 %copy-start.9 = (f32[32,2,256]{2,0,1:T(8,128)S(1)}, f32[32,2,256]{2,0,1:T(8,128)}, u32[]{:S(2)}) copy-start(f32[32,2,256]{2,0,1:T(8,128)} %constant.51.clone) | copy-start | bytes 196612
  55.3 28.1 %copy-start.5 = (f32[128,128]{1,0:T(8,128)S(1)}, f32[128,128]{1,0:T(8,128)}, u32[]{:S(2)}) copy-start(f32[128,128]{1,0:T(8,128)} %beam.3) | copy-start | bytes 196612
  55.3 28.1 %copy-start.6 = (s32[64,64]{1,0:T(8,128)S(1)}, s32[64,64]{1,0:T(8,128)}, u32[]{:S(2)}) copy-start(s32[64,64]{1,0:T(8,128)} %pointing.3) | copy-start | bytes 49156
  77.7 1.3 copy-start.7
  79.0 114.6 %all-to-all-start.1 = ((f32[32,128,256]{2,1,0:T(8,128)}), f32[32,128,256]{2,1,0:T(8,128)}, u32[]{:S(2)}, u32[]{:S(2)}) async-start(f32[32,128,256]{2,1,0:T(8,128)} %sky_forward.1), calls=%async_computation.1 | async-start | bytes 8388608 | tf_op jit(solution)/shard_map/all_to_all | solution.py:431
  82.8 76.4 %all-reduce.2.cloned.1.call-start = ((), (), s32[]{:S(2)}) async-start(), calls=%async_computation.5 | async-start | bytes 1048576 | tf_op jit(solution)/shard_map/psum | solution.py:467
  83.3 35.7 %copy-start.8 = (f32[32,16,16]{0,2,1:T(8,128)S(1)}, f32[32,16,16]{0,2,1:T(8,128)}, u32[]{:S(2)}) copy-start(f32[32,16,16]{0,2,1:T(8,128)} %param.28) | copy-start | bytes 98308
  83.3 35.7 %copy-start.10 = (f32[32,2,256,1]{2,0,3,1:T(8,128)S(1)}, f32[32,2,256,1]{2,0,3,1:T(8,128)}, u32[]{:S(2)}) copy-start(f32[32,2,256,1]{2,0,3,1:T(8,128)} %constant.56) | copy-start | bytes 196612
  117.7 1.3 copy-start.3
  159.2 1.0 copy-start.4
  193.7 55.2 %all-to-all-start.4 = ((f32[8,4,128,128]{3,2,1,0:T(8,128)}), f32[8,4,128,128]{3,2,1,0:T(8,128)S(1)}, u32[]{:S(2)}, u32[]{:S(2)}) async-start(f32[8,4,128,128]{3,2,1,0:T(8,128)} %bitcast.12), calls=%async_computation.4 | async-start | bytes 4194304 | tf_op jit(solution)/shard_map/all_to_all | solution.py:494
  202.9 1.6 copy-start.2
  347.4 25.0 %copy-start.1 = (f32[64,32]{0,1:T(8,128)S(1)}, f32[64,32]{0,1:T(8,128)}, u32[]{:S(2)}) copy-start(f32[64,32]{0,1:T(8,128)} %param.26) | copy-start | bytes 24580
Sparse Core Ops, SparseCore 0:
  119.2 39.9 all-reduce.1

commit v2 on v1

--- a/solution.py
+++ b/solution.py
@@ -12,6 +12,7 @@
 
 BAND_WIDTH = 128
 LANES = 128
+BATCH = 4
 LIMIT = 50 * 1024 * 1024
 F32 = jnp.float32
 BF16 = jnp.bfloat16
@@ -156,25 +157,26 @@
 
 def sky_forward_kernel(sky, high, low, out, held):
     rows, width = sky.shape
-    group = pl.program_id(0)
-
-    @pl.when(group == 0)
+    step = pl.program_id(0)
+
+    @pl.when(step == 0)
     def _():
         def load(tile, at):
             return sky[at, tile * LANES : (tile + 1) * LANES]
 
         rows_forward(load, held, rows, width // LANES)
 
-    out[0] = multiply(split(held[group]), (high[0], low[0]))
+    for i in range(BATCH):
+        out[i] = multiply(split(held[step * BATCH + i]), (high[i], low[i]))
 
 
 def column_kernel(cols, row_sq, col_sq, f_high, f_low, b_high, b_low, out, held, *, knee_sq):
     length, width = cols.shape
     outer = length // LANES
-    group = pl.program_id(0)
+    step = pl.program_id(0)
     chunks = [(at, min(LANES, width)) for at in range(0, width, LANES)]
 
-    @pl.when(group == 0)
+    @pl.when(step == 0)
     def _():
         def body(index, carry):
             first = pl.multiple_of(index * 8, 8)
@@ -195,12 +197,14 @@
 
         lax.fori_loop(0, LANES // 8, body, 0)
 
-    spectrum = multiply((f_high[0], f_low[0]), split(held[group]))
-    radial_sq = row_sq[0] + col_sq[...]
-    gain = 1.0 + radial_sq * 20.0 + 0.25 * lax.rsqrt(radial_sq + knee_sq)
-    held[group] = multiply((b_high[0], b_low[0]), split(spectrum * gain))
-
-    @pl.when(group == pl.num_programs(0) - 1)
+    for i in range(BATCH):
+        group = step * BATCH + i
+        spectrum = multiply((f_high[i], f_low[i]), split(held[group]))
+        radial_sq = row_sq[i] + col_sq[...]
+        gain = 1.0 + radial_sq * 20.0 + 0.25 * lax.rsqrt(radial_sq + knee_sq)
+        held[group] = multiply((b_high[i], b_low[i]), split(spectrum * gain))
+
+    @pl.when(step == pl.num_programs(0) - 1)
     def _():
         def body(index, carry):
             first = pl.multiple_of(index * 8, 8)
@@ -221,29 +225,34 @@
         lax.fori_loop(0, LANES // 8, body, 0)
 
 
-def finish_kernel(ids, spectrum, high, low, delivered, out, held):
+def sky_backward_kernel(spectrum, high, low, out, held):
     rows, width = out.shape
-    group = pl.program_id(0)
-    held[group] = multiply(split(spectrum[0]), (high[0], low[0]))
-
-    @pl.when(group == pl.num_programs(0) - 1)
+    step = pl.program_id(0)
+    for i in range(BATCH):
+        held[step * BATCH + i] = multiply(split(spectrum[i]), (high[i], low[i]))
+
+    @pl.when(step == pl.num_programs(0) - 1)
     def _():
         def store(tile, at, value):
             out[at, tile * LANES : (tile + 1) * LANES] = -value
 
         rows_backward(store, held, rows, width // LANES)
 
-        def body(slot, carry):
-            block = ids[slot]
-
-            @pl.when(block < width // LANES)
-            def _():
-                at = pl.ds(pl.multiple_of(block * LANES, LANES), LANES)
-                out[:, at] = out[:, at] + delivered[slot]
-
-            return carry
-
-        lax.fori_loop(0, delivered.shape[0], body, 0)
+
+def finish_kernel(ids, base, delivered, out):
+    out[...] = base[...]
+
+    def body(slot, carry):
+        block = ids[slot]
+
+        @pl.when(block < out.shape[1] // LANES)
+        def _():
+            at = pl.ds(pl.multiple_of(block * LANES, LANES), LANES)
+            out[:, at] = out[:, at] + delivered[slot]
+
+        return carry
+
+    lax.fori_loop(0, delivered.shape[0], body, 0)
 
 
 def data_forward_kernel(
@@ -252,9 +261,9 @@
     dets, width = data.shape
     outer = width // LANES
     wanted, block_rows = slots.shape[0], arrived.shape[1]
-    group = pl.program_id(0)
-
-    @pl.when(group == 0)
+    step = pl.program_id(0)
+
+    @pl.when(step == 0)
     def _():
         def place(entry, carry):
             at = pl.ds(pl.multiple_of(entry * block_rows, 8), block_rows)
@@ -277,9 +286,12 @@
 
         rows_forward(lambda tile, at: tiles[tile, at, :], held, dets, outer)
 
-    spec = multiply(split(held[group]), (high[0], low[0]))
-    spec_out[0] = spec
-    proj_out[0] = multiply(split(loading[...]), split(white[0] * spec), (((0,), (0,)), ((), ())))
+    for i in range(BATCH):
+        group = step * BATCH + i
+        spec = multiply(split(held[group]), (high[i], low[i]))
+        spec_out[i] = spec
+        weighted = white[jnp.minimum(group, 1)] * spec
+        proj_out[i] = multiply(split(loading[...]), split(weighted), (((0,), (0,)), ((), ())))
 
 
 def data_backward_kernel(
@@ -289,15 +301,18 @@
     modes = proj.shape[1]
     outer = tiles.shape[0]
     wanted, block_rows = slots.shape[0], out.shape[1]
-    group = pl.program_id(0)
-    coupled = coupling[0, 0] * proj[0, 0:1, :]
-    for mode in range(1, modes):
-        coupled = coupled + coupling[0, mode] * proj[0, mode : mode + 1, :]
-    common = multiply(split(loading[...]), split(coupled))
-    filtered = white[0] * (spec[0] - common)
-    held[group] = multiply(split(filtered), (high[0], low[0]))
-
-    @pl.when(group == pl.num_programs(0) - 1)
+    step = pl.program_id(0)
+    for i in range(BATCH):
+        group = step * BATCH + i
+        kind = jnp.minimum(group, 1)
+        coupled = coupling[kind, 0] * proj[i, 0:1, :]
+        for mode in range(1, modes):
+            coupled = coupled + coupling[kind, mode] * proj[i, mode : mode + 1, :]
+        common = multiply(split(loading[...]), split(coupled))
+        filtered = white[kind] * (spec[i] - common)
+        held[group] = multiply(split(filtered), (high[i], low[i]))
+
+    @pl.when(step == pl.num_programs(0) - 1)
     def _():
         def store(tile, at, value):
             tiles[tile, at, :] = value
@@ -336,13 +351,7 @@
 
 
 def sliced(array):
-    return pl.BlockSpec((1,) + array.shape[1:], lambda g, n=len(array.shape): (g,) + (0,) * (n - 1))
-
-
-def first_or_rest(array):
-    return pl.BlockSpec(
-        (1,) + array.shape[1:], lambda g, n=len(array.shape): (jnp.minimum(g, 1),) + (0,) * (n - 1)
-    )
+    return pl.BlockSpec((BATCH,) + array.shape[1:], lambda g, n=len(array.shape): (g,) + (0,) * (n - 1))
 
 
 PARAMS = pltpu.CompilerParams(vmem_limit_bytes=LIMIT)
@@ -398,9 +407,8 @@
     slot_index = target * capacity + jnp.sum(earlier.astype(jnp.int32), axis=1)
     named = slot_index[None, :] == jnp.arange(slots, dtype=jnp.int32)[:, None]
     send_ids = blocks_here + jnp.sum(jnp.where(named, request_block[None, :] - blocks_here, 0), axis=1)
-    asked_ids = lax.all_to_all(
-        send_ids.reshape(owners, capacity), "tm", split_axis=0, concat_axis=0, tiled=True
-    ).reshape(-1)
+    all_ids = lax.all_gather(send_ids, "tm", axis=0).reshape(owners, owners, capacity)
+    asked_ids = lax.dynamic_index_in_dim(all_ids, lax.axis_index("tm"), 1, False).reshape(-1)
 
     outgoing = pl.pallas_call(
         pick_kernel,
@@ -410,15 +418,11 @@
         compiler_params=PARAMS,
         name="pick_blocks",
     )(asked_ids, sky_map)
-    arrived = lax.all_to_all(
-        outgoing.reshape(owners, capacity, rows_here, tile), "tm", split_axis=0, concat_axis=0, tiled=True
-    ).reshape(slots, rows_here, tile)
-
     packed = pl.pallas_call(
         sky_forward_kernel,
-        grid=(groups,),
+        grid=(groups // BATCH,),
         in_specs=[whole(sky_map), sliced(row_forward[0]), sliced(row_forward[1])],
-        out_specs=pl.BlockSpec((1, rows_here, wide), lambda g: (g, 0, 0)),
+        out_specs=pl.BlockSpec((BATCH, rows_here, wide), lambda g: (g, 0, 0)),
         out_shape=struct(groups, rows_here, wide),
         scratch_shapes=[pltpu.VMEM((groups, rows_here, wide), F32)],
         compiler_params=PARAMS,
@@ -429,70 +433,10 @@
         packed = packed.reshape(groups, rows_here, parts, per_device).transpose(0, 2, 1, 3)
         packed = packed.reshape(devices, rows_here, per_device)
     columns = lax.all_to_all(packed, ("det", "tm"), split_axis=0, concat_axis=0, tiled=True)
+    columns, outgoing = lax.optimization_barrier((columns, outgoing))
     columns = columns.reshape(total_rows, per_device)
-
-    freq = group_frequencies(samples)[:2]
-    band = np.minimum(np.minimum(freq, samples - freq) // BAND_WIDTH, bands - 1)
-    onehot = jnp.asarray((np.arange(bands)[:, None, None] == band[None]).astype(np.float32))
-    precise = lax.Precision.HIGHEST
-    white = jnp.einsum("jb,bgf->gjf", inv_white, onehot, precision=precise)
-    coupling = jnp.einsum("bmn,bgf->gnmf", mode_kernel, onehot, precision=precise)
-    spec, proj = pl.pallas_call(
-        data_forward_kernel,
-        grid=(time_groups,),
-        in_specs=[
-            SCALARS,
-            SCALARS,
-            whole(arrived),
-            whole(detector_data),
-            whole(beam_kernel),
-            first_or_rest(white),
-            whole(mode_loading),
-            sliced(time_forward[0]),
-            sliced(time_forward[1]),
-        ],
-        out_specs=[
-            pl.BlockSpec((1, dets, wide), lambda g: (g, 0, 0)),
-            pl.BlockSpec((1, modes, wide), lambda g: (g, 0, 0)),
-        ],
-        out_shape=[struct(time_groups, dets, wide), struct(time_groups, modes, wide)],
-        scratch_shapes=[
-            pltpu.VMEM((time_groups, dets, wide), F32),
-            pltpu.VMEM((wanted * rows_here, tile), F32),
-            pltpu.VMEM((samples // tile, dets, tile), F32),
-        ],
-        compiler_params=PARAMS,
-        name="data_forward",
-    )(pointing, slot_index, arrived, detector_data, beam_kernel, white, mode_loading, *time_forward)
-    proj = lax.psum(proj, "det")
-
-    returned = pl.pallas_call(
-        data_backward_kernel,
-        grid=(time_groups,),
-        in_specs=[
-            SCALARS,
-            SCALARS,
-            sliced(spec),
-            sliced(proj),
-            first_or_rest(coupling),
-            whole(beam_kernel),
-            first_or_rest(white),
-            whole(mode_loading),
-            sliced(time_backward[0]),
-            sliced(time_backward[1]),
-        ],
-        out_specs=pl.BlockSpec((slots, rows_here, tile), lambda g: (0, 0, 0)),
-        out_shape=struct(slots, rows_here, tile),
-        scratch_shapes=[
-            pltpu.VMEM((time_groups, dets, wide), F32),
-            pltpu.VMEM((samples // tile, dets, tile), F32),
-        ]
-        + [pltpu.VMEM((wanted * rows_here, tile), F32)] * 4,
-        compiler_params=PARAMS,
-        name="data_backward",
-    )(pointing, slot_index, spec, proj, coupling, beam_kernel, white, mode_loading, *time_backward)
-    delivered = lax.all_to_all(
-        returned.reshape(owners, capacity, rows_here, tile), "tm", split_axis=0, concat_axis=0, tiled=True
+    arrived = lax.all_to_all(
+        outgoing.reshape(owners, capacity, rows_here, tile), "tm", split_axis=0, concat_axis=0, tiled=True
     ).reshape(slots, rows_here, tile)
 
     rank = lax.axis_index("det") * owners + lax.axis_index("tm")
@@ -507,7 +451,7 @@
     knee_sq = 1.0 / (2.0 * math.pi * total_rows / 64.0) ** 2
     backed = pl.pallas_call(
         functools.partial(column_kernel, knee_sq=knee_sq),
-        grid=(col_groups,),
+        grid=(col_groups // BATCH,),
         in_specs=[whole(columns), sliced(row_sq), whole(col_sq)]
         + [sliced(t) for t in col_forward + col_backward],
         out_specs=pl.BlockSpec((total_rows, per_device), lambda g: (0, 0)),
@@ -516,6 +460,7 @@
         compiler_params=PARAMS,
         name="sky_columns",
     )(columns, row_sq, col_sq, *col_forward, *col_backward)
+    backed, arrived = lax.optimization_barrier((backed, arrived))
     spectrum = lax.all_to_all(
         backed.reshape(devices, rows_here, per_device),
         ("det", "tm"),
@@ -527,22 +472,96 @@
         spectrum = spectrum.reshape(groups, parts, rows_here, per_device).transpose(0, 2, 1, 3)
         spectrum = spectrum.reshape(groups, rows_here, wide)
 
-    return pl.pallas_call(
-        finish_kernel,
-        grid=(groups,),
+    freq = group_frequencies(samples)[:2]
+    band = np.minimum(np.minimum(freq, samples - freq) // BAND_WIDTH, bands - 1)
+    onehot = jnp.asarray((np.arange(bands)[:, None, None] == band[None]).astype(np.float32))
+    precise = lax.Precision.HIGHEST
+    white = jnp.einsum("jb,bgf->gjf", inv_white, onehot, precision=precise)
+    coupling = jnp.einsum("bmn,bgf->gnmf", mode_kernel, onehot, precision=precise)
+    spec, proj = pl.pallas_call(
+        data_forward_kernel,
+        grid=(time_groups // BATCH,),
         in_specs=[
             SCALARS,
-            sliced(spectrum),
-            sliced(row_backward[0]),
-            sliced(row_backward[1]),
-            whole(delivered),
+            SCALARS,
+            whole(arrived),
+            whole(detector_data),
+            whole(beam_kernel),
+            whole(white),
+            whole(mode_loading),
+            sliced(time_forward[0]),
+            sliced(time_forward[1]),
         ],
+        out_specs=[
+            pl.BlockSpec((BATCH, dets, wide), lambda g: (g, 0, 0)),
+            pl.BlockSpec((BATCH, modes, wide), lambda g: (g, 0, 0)),
+        ],
+        out_shape=[struct(time_groups, dets, wide), struct(time_groups, modes, wide)],
+        scratch_shapes=[
+            pltpu.VMEM((time_groups, dets, wide), F32),
+            pltpu.VMEM((wanted * rows_here, tile), F32),
+            pltpu.VMEM((samples // tile, dets, tile), F32),
+        ],
+        compiler_params=PARAMS,
+        name="data_forward",
+    )(pointing, slot_index, arrived, detector_data, beam_kernel, white, mode_loading, *time_forward)
+    proj = lax.psum(proj, "det")
+
+    returned = pl.pallas_call(
+        data_backward_kernel,
+        grid=(time_groups // BATCH,),
+        in_specs=[
+            SCALARS,
+            SCALARS,
+            sliced(spec),
+            sliced(proj),
+            whole(coupling),
+            whole(beam_kernel),
+            whole(white),
+            whole(mode_loading),
+            sliced(time_backward[0]),
+            sliced(time_backward[1]),
+        ],
+        out_specs=pl.BlockSpec((slots, rows_here, tile), lambda g: (0, 0, 0)),
+        out_shape=struct(slots, rows_here, tile),
+        scratch_shapes=[
+            pltpu.VMEM((time_groups, dets, wide), F32),
+            pltpu.VMEM((samples // tile, dets, tile), F32),
+        ]
+        + [pltpu.VMEM((wanted * rows_here, tile), F32)] * 4,
+        compiler_params=PARAMS,
+        name="data_backward",
+    )(pointing, slot_index, spec, proj, coupling, beam_kernel, white, mode_loading, *time_backward)
+    returned, spectrum = lax.optimization_barrier((returned, spectrum))
+    delivered = lax.all_to_all(
+        returned.reshape(owners, capacity, rows_here, tile), "tm", split_axis=0, concat_axis=0, tiled=True
+    ).reshape(slots, rows_here, tile)
+
+    base = pl.pallas_call(
+        sky_backward_kernel,
+        grid=(groups // BATCH,),
+        in_specs=[sliced(spectrum), sliced(row_backward[0]), sliced(row_backward[1])],
         out_specs=pl.BlockSpec((rows_here, map_cols), lambda g: (0, 0)),
         out_shape=struct(rows_here, map_cols),
         scratch_shapes=[pltpu.VMEM((groups, rows_here, wide), F32)],
         compiler_params=PARAMS,
+        name="sky_backward",
+    )(spectrum, *row_backward)
+
+    chunk = rows_here // 4
+    return pl.pallas_call(
+        finish_kernel,
+        grid=(4,),
+        in_specs=[
+            SCALARS,
+            pl.BlockSpec((chunk, map_cols), lambda g: (g, 0)),
+            pl.BlockSpec((slots, chunk, tile), lambda g: (0, g, 0)),
+        ],
+        out_specs=pl.BlockSpec((chunk, map_cols), lambda g: (g, 0)),
+        out_shape=struct(rows_here, map_cols),
+        compiler_params=PARAMS,
         name="sky_finish",
-    )(asked_ids, spectrum, *row_backward, delivered)
+    )(asked_ids, base, delivered)
 
 
 def solution(mesh):

time: 382 us -> 358 us (0.937)
  Pallas kernels: 143 us -> 87.9 us
  waiting for transfers between devices: 85 us -> 115 us
    unnamed x0 -> x1, blocking collectives: none -> 115 us
    all_to_all x2 -> x0, blocking collectives: 112 us -> none  [the longest x1 98.5 us: local(): lax.all_to_all(backed.reshape(devices, rows_here, per_device), ('det', 't...]
    pallas_call x4 -> x5, Pallas kernels: 117 us -> 70 us  [the longest x1 22 us: local(): pl.pallas_call(data_forward_kernel, grid=(time_groups // BATCH,), in_spec...]
    all_to_all x1, waiting for transfers between devices: 23 us -> 36.7 us  [local(): lax.all_to_all(returned.reshape(owners, capacity, rows_here, tile), 'tm',...]
    all_to_all x0 -> x1, waiting for transfers between devices: none -> 9.87 us  [local(): lax.all_to_all(backed.reshape(devices, rows_here, per_device), ('det', 't...]
    pallas_call x1, Pallas kernels: 21.5 us -> 13.7 us  [local(): pl.pallas_call(functools.partial(column_kernel, knee_sq=knee_sq), grid=(c...]
    all_to_all x1, waiting for transfers between devices: 22.4 us -> 27.7 us  [local(): lax.all_to_all(outgoing.reshape(owners, capacity, rows_here, tile), 'tm',...]
    all_to_all x1, starting transfers between devices: 8.5 us -> 3.6 us  [local(): lax.all_to_all(returned.reshape(owners, capacity, rows_here, tile), 'tm',...]
  transfers between devices with their start and end apart: 4 -> 5, of which waited for: 3 -> 4; matrix products, arithmetic and copies ran while one was open for 0% -> 1% of each run, Pallas kernels for 30% -> 20%
where the time goes in v2:
time: 358 us; the launch traced here: 357 us
  blocking collectives  115 us (32%)
  waiting for transfers between devices  115 us (32%)
  Pallas kernels  87.9 us (25%)
  starting transfers between devices  19.5 us (5%)
  between operations  14.3 us (4%)
  local copies, waits for them, and re-layouts  4.07 us (1%)
    unnamed x1, blocking collectives  115 us
    psum x1, waiting for transfers between devices, local(): proj = lax.psum(proj, 'det')  40.6 us
    all_to_all x1, waiting for transfers between devices, local(): lax.all_to_all(returned.reshape(owners, capacity, rows_here, tile), 'tm',...  36.7 us
    all_to_all x1, waiting for transfers between devices, local(): lax.all_to_all(outgoing.reshape(owners, capacity, rows_here, tile), 'tm',...  27.7 us
    pallas_call x1, Pallas kernels, local(): pl.pallas_call(data_forward_kernel, grid=(time_groups // BATCH,), in_spec...  22 us
    pallas_call x1, Pallas kernels, local(): pl.pallas_call(data_backward_kernel, grid=(time_groups // BATCH,), in_spe...  19.2 us
    pallas_call x1, Pallas kernels, local(): pl.pallas_call(functools.partial(column_kernel, knee_sq=knee_sq), grid=(c...  13.7 us
    pallas_call x1, Pallas kernels, local(): pl.pallas_call(sky_forward_kernel, grid=(groups // BATCH,), in_specs=[who...  11.6 us
  transfers between devices with their start and end apart: 5, of which 4 were waited for; matrix products, arithmetic and copies ran while one was open for 1% of the time, Pallas kernels for 20%

profile of v2, /device:TPU:0, one launch (start us, length us, event | category | flops | bytes accessed | tf_op | source)
XLA Modules:
  0.0 356.9 jit_solution(11869664112667803312)
XLA Ops:
  6.5 0.0 copy-start
  6.5 11.6 %sky_forward.1 = f32[32,128,256]{2,1,0:T(8,128)} custom-call(f32[128,8192]{1,0:T(8,128)} %sky.3, bf16[32,256,256]{2,1,0:T(8,128)(2,1)} %constant.47.clone.high, bf16[32,256,256]{2,1,0:T(8,128)(2,1)} %constant.48.clone.low), custom_call_target="tpu_custom_call" | custom-call | tf_op jit(solution)/shard_map/sky_forward/pallas_call | solution.py:421
  18.1 0.0 copy-start.13
  18.1 0.0 copy-start.11
  18.1 0.0 copy-start.12
  18.1 7.4 %all-to-all-start = ((f32[32,128,256]{2,1,0:T(8,128)}), f32[32,128,256]{2,1,0:T(8,128)}, u32[]{:S(2)}, u32[]{:S(2)}) async-start(f32[32,128,256]{2,1,0:T(8,128)} %sky_forward.1), calls=%async_computation | async-start | bytes 8388608 | tf_op jit(solution)/shard_map/all_to_all | solution.py:435
  25.6 0.0 copy-done.13
  25.6 0.7 dynamic-slice
  26.9 0.0 copy-done.11
  26.9 0.2 convert_reduce_fusion
  27.1 0.0 copy-done.12
  27.1 0.1 select_reduce_fusion
  27.2 0.1 add_dynamic-update-slice_fusion
  27.3 0.1 reshape.45
  27.4 115.0 %all-reduce.1 = s32[8,8,4]{2,1,0:T(8,128)S(1)} all-reduce(s32[8,8,4]{2,1,0:T(8,128)S(1)} %reshape.45), channel_id=2, replica_groups=mesh['det'=4,'tm'=8] {'tm'}, use_global_device_ids=true, to_apply=%add | all-reduce | flops 256 | bytes 2048
  142.4 0.1 reshape.46.ids
  142.5 0.0 copy-start.2
  142.5 4.2 %pick_blocks.1 = f32[32,128,128]{2,1,0:T(8,128)} custom-call(s32[32]{0:T(128)S(1)} %reshape.46.ids, f32[128,8192]{1,0:T(8,128)} %sky.3), custom_call_target="tpu_custom_call" | custom-call | tf_op jit(solution)/shard_map/pick_blocks/pallas_call | solution.py:413
  146.7 0.0 all-to-all-done
  146.7 4.3 %all-to-all-start.1 = ((f32[8,4,128,128]{3,2,1,0:T(8,128)}), f32[8,4,128,128]{3,2,1,0:T(8,128)}, u32[]{:S(2)}, u32[]{:S(2)}) async-start(f32[8,4,128,128]{3,2,1,0:T(8,128)} %bitcast.3), calls=%async_computation.1 | async-start | bytes 4194304 | tf_op jit(solution)/shard_map/all_to_all | solution.py:438
  151.1 0.7 constant_dynamic-slice_fusion.col_sq
  151.8 0.0 copy-done.2
  151.8 13.7 %sky_columns.1 = f32[4096,256]{1,0:T(8,128)} custom-call(f32[4096,256]{1,0:T(8,128)} %bitcast.2.cols, f32[16,256,1]{2,1,0:T(8,128)S(1)} %copy-done.2, f32[1,256]{1,0:T(1,128)S(1)} %constant_dynamic-slice_fusion.col_sq, bf16[16,256,256]{2,1,0:T(8,128)(2,1)} %constant.51.clone.f_high, bf16[16,256,256]{2,1,0:T(8,128)(2,1)} %constant.52.clone.f_low, ...), custom_call_target="tpu_custom_call" | custom-call | tf_op jit(solution)/shard_map/sky_columns/pallas_call | solution.py:452
  165.5 27.7 %all-to-all-done.1 = f32[8,4,128,128]{3,2,1,0:T(8,128)} async-done(((f32[8,4,128,128]{3,2,1,0:T(8,128)}), f32[8,4,128,128]{3,2,1,0:T(8,128)}, u32[]{:S(2)}, u32[]{:S(2)}) %all-to-all-start.1) | async-done | bytes 2097184 | tf_op jit(solution)/shard_map/all_to_all | solution.py:438
  193.2 0.0 copy-start.10
  193.2 0.0 copy-start.8
  193.2 0.0 copy-start.5
  193.2 0.0 copy-start.6
  193.2 4.1 %all-to-all-start.2 = ((f32[32,128,256]{2,1,0:T(8,128)}), f32[32,128,256]{2,1,0:T(8,128)}, u32[]{:S(2)}, u32[]{:S(2)}) async-start(f32[32,128,256]{2,1,0:T(8,128)} %bitcast.25), calls=%async_computation.2 | async-start | bytes 8388608 | tf_op jit(solution)/shard_map/all_to_all | solution.py:464
  197.3 0.0 all-reduce.4.cloned.1.call-start
  197.3 0.0 copy-done.10
  197.3 0.1 copy.27.loading
  197.4 0.0 copy-done
  197.4 0.0 copy-done.8
  197.4 0.3 convolution_bitcast_fusion.1.white
  197.8 0.0 copy-done.5
  197.8 0.0 copy-done.6
  197.8 0.0 copy-start.7
  197.8 0.0 copy-start.9
  197.8 22.0 %data_forward.1 = (f32[32,64,256]{2,1,0:T(8,128)S(1)}, f32[32,16,256]{2,1,0:T(8,128)}) custom-call(s32[64,64]{1,0:T(8,128)S(1)} %copy-done.6, s32[16]{0:T(128)S(1)} %get-tuple-element.21.slots, f32[32,128,128]{2,1,0:T(8,128)} %bitcast.4.arrived, f32[64,8192]{1,0:T(8,128)} %data.1, f32[128,128]{1,0:T(8,128)S(1)} %copy-done.5, ...), custom_call_target="tpu_custom_call" | custom-call | tf_op jit(solution)/shard_map/data_forward/pallas_call | solution.py:481
  219.8 0.0 copy-start.3
  219.8 1.3 copy-done.3
  221.1 0.0 all-reduce.4.cloned.1.call-update
  221.1 0.0 copy-done.7
  221.1 0.0 copy-done.9
  221.1 0.6 convolution_bitcast_fusion.coupling
  221.7 40.6 %all-reduce.4.cloned.1.call-done.proj = f32[32,16,256]{2,1,0:T(8,128)} async-done(((f32[32,16,256]{2,1,0:T(8,128)}), f32[32,16,256]{2,1,0:T(8,128)}) %all-reduce.4.cloned.1.call-update) | async-done | bytes 524304 | tf_op jit(solution)/shard_map/psum | solution.py:508
  262.3 0.0 copy-start.4
  262.3 1.0 copy-done.4
  263.4 19.2 %data_backward.1 = f32[32,128,128]{2,1,0:T(8,128)} custom-call(s32[64,64]{1,0:T(8,128)S(1)} %copy-done.6, s32[16]{0:T(128)S(1)} %get-tuple-element.21.slots, f32[32,64,256]{2,1,0:T(8,128)} %copy-done.3, f32[32,16,256]{2,1,0:T(8,128)S(1)} %copy-done.4, f32[2,16,16,256]{3,2,1,0:T(8,128)S(1)} %convolution_bitcast_fusion.coupling, f32[128,128]{1,0:T(8,128)S(1)} %copy-done.5, ...), custom_call_target="tpu_custom_call" | custom-call | tf_op jit(solution)/shard_map/data_backward/pallas_call | solution.py:510
  282.6 9.9 %all-to-all-done.2.spectrum = f32[32,128,256]{2,1,0:T(8,128)} async-done(((f32[32,128,256]{2,1,0:T(8,128)}), f32[32,128,256]{2,1,0:T(8,128)}, u32[]{:S(2)}, u32[]{:S(2)}) %all-to-all-start.2) | async-done | bytes 4194336 | tf_op jit(solution)/shard_map/all_to_all | solution.py:464
  292.4 3.6 %all-to-all-start.3 = ((f32[8,4,128,128]{3,2,1,0:T(8,128)}), f32[8,4,128,128]{3,2,1,0:T(8,128)S(1)}, u32[]{:S(2)}, u32[]{:S(2)}) async-start(f32[8,4,128,128]{3,2,1,0:T(8,128)} %bitcast.12), calls=%async_computation.3 | async-start | bytes 4194304 | tf_op jit(solution)/shard_map/all_to_all | solution.py:536
  296.0 11.6 %sky_backward.1.base = f32[128,8192]{1,0:T(8,128)} custom-call(f32[32,128,256]{2,1,0:T(8,128)} %all-to-all-done.2.spectrum, bf16[32,256,256]{2,1,0:T(8,128)(2,1)} %constant.49.clone.high, bf16[32,256,256]{2,1,0:T(8,128)(2,1)} %constant.50.clone.low), custom_call_target="tpu_custom_call" | custom-call | tf_op jit(solution)/shard_map/sky_backward/pallas_call | solution.py:540
  307.6 36.7 %all-to-all-done.3 = f32[8,4,128,128]{3,2,1,0:T(8,128)S(1)} async-done(((f32[8,4,128,128]{3,2,1,0:T(8,128)}), f32[8,4,128,128]{3,2,1,0:T(8,128)S(1)}, u32[]{:S(2)}, u32[]{:S(2)}) %all-to-all-start.3) | async-done | bytes 2097184 | tf_op jit(solution)/shard_map/all_to_all | solution.py:536
  344.3 0.0 copy-start.1
  344.3 5.7 %sky_finish.1 = f32[128,8192]{1,0:T(8,128)} custom-call(s32[32]{0:T(128)S(1)} %reshape.46.ids, f32[128,8192]{1,0:T(8,128)} %sky_backward.1.base, f32[32,128,128]{2,1,0:T(8,128)S(1)} %bitcast.24), custom_call_target="tpu_custom_call" | custom-call | tf_op jit(solution)/shard_map/sky_finish/pallas_call | solution.py:552
  350.0 0.0 copy-done.1
  (3 shorter events, 0.0 us)
Async XLA Ops:
  6.5 190.9 %copy-start = (f32[64,32]{0,1:T(8,128)S(1)}, f32[64,32]{0,1:T(8,128)}, u32[]{:S(2)}) copy-start(f32[64,32]{0,1:T(8,128)} %param.26) | copy-start | bytes 24580
  18.1 7.5 %copy-start.13 = (u32[32]{0:T(128)S(1)}, u32[32]{0:T(128)}, u32[]{:S(2)}) copy-start(u32[32]{0:T(128)} %constant.62) | copy-start | bytes 388
  18.1 8.8 %copy-start.11 = (s32[16,1]{0,1:T(1,128)S(1)}, s32[16,1]{0,1:T(1,128)}, u32[]{:S(2)}) copy-start(s32[16,1]{0,1:T(1,128)} %param.23) | copy-start | bytes 196
  18.1 9.0 %copy-start.12 = (s32[16]{0:T(128)S(1)}, s32[16]{0:T(128)}, u32[]{:S(2)}) copy-start(s32[16]{0:T(128)} %param.24) | copy-start | bytes 196
  18.1 128.6 %all-to-all-start = ((f32[32,128,256]{2,1,0:T(8,128)}), f32[32,128,256]{2,1,0:T(8,128)}, u32[]{:S(2)}, u32[]{:S(2)}) async-start(f32[32,128,256]{2,1,0:T(8,128)} %sky_forward.1), calls=%async_computation | async-start | bytes 8388608 | tf_op jit(solution)/shard_map/all_to_all | solution.py:435
  142.5 9.3 %copy-start.2 = (f32[16,256,1]{2,1,0:T(8,128)S(1)}, f32[16,256,1]{2,1,0:T(8,128)}, u32[]{:S(2)}) copy-start(f32[16,256,1]{2,1,0:T(8,128)} %constant.56.clone.row_sq) | copy-start | bytes 49156
  146.7 46.5 %all-to-all-start.1 = ((f32[8,4,128,128]{3,2,1,0:T(8,128)}), f32[8,4,128,128]{3,2,1,0:T(8,128)}, u32[]{:S(2)}, u32[]{:S(2)}) async-start(f32[8,4,128,128]{3,2,1,0:T(8,128)} %bitcast.3), calls=%async_computation.1 | async-start | bytes 4194304 | tf_op jit(solution)/shard_map/all_to_all | solution.py:438
  193.2 4.1 %copy-start.10 = (f32[64,16]{0,1:T(8,128)S(1)}, f32[64,16]{0,1:T(8,128)}, u32[]{:S(2)}) copy-start(f32[64,16]{0,1:T(8,128)} %param.27) | copy-start | bytes 12292
  193.2 4.2 %copy-start.8 = (f32[32,2,256]{2,0,1:T(8,128)S(1)}, f32[32,2,256]{2,0,1:T(8,128)}, u32[]{:S(2)}) copy-start(f32[32,2,256]{2,0,1:T(8,128)} %constant.57.clone) | copy-start | bytes 196612
  193.2 4.6 %copy-start.5 = (f32[128,128]{1,0:T(8,128)S(1)}, f32[128,128]{1,0:T(8,128)}, u32[]{:S(2)}) copy-start(f32[128,128]{1,0:T(8,128)} %beam.3) | copy-start | bytes 196612
  193.2 4.6 %copy-start.6 = (s32[64,64]{1,0:T(8,128)S(1)}, s32[64,64]{1,0:T(8,128)}, u32[]{:S(2)}) copy-start(s32[64,64]{1,0:T(8,128)} %pointing.3) | copy-start | bytes 49156
  193.2 99.2 %all-to-all-start.2 = ((f32[32,128,256]{2,1,0:T(8,128)}), f32[32,128,256]{2,1,0:T(8,128)}, u32[]{:S(2)}, u32[]{:S(2)}) async-start(f32[32,128,256]{2,1,0:T(8,128)} %bitcast.25), calls=%async_computation.2 | async-start | bytes 8388608 | tf_op jit(solution)/shard_map/all_to_all | solution.py:464
  197.3 65.0 %all-reduce.4.cloned.1.call-start = ((), (), s32[]{:S(2)}) async-start(), calls=%async_computation.4 | async-start | bytes 1048576 | tf_op jit(solution)/shard_map/psum | solution.py:508
  197.8 23.3 %copy-start.7 = (f32[32,16,16]{0,2,1:T(8,128)S(1)}, f32[32,16,16]{0,2,1:T(8,128)}, u32[]{:S(2)}) copy-start(f32[32,16,16]{0,2,1:T(8,128)} %param.28) | copy-start | bytes 98308
  197.8 23.3 %copy-start.9 = (f32[32,2,256,1]{2,0,3,1:T(8,128)S(1)}, f32[32,2,256,1]{2,0,3,1:T(8,128)}, u32[]{:S(2)}) copy-start(f32[32,2,256,1]{2,0,3,1:T(8,128)} %constant.66) | copy-start | bytes 196612
  219.8 1.3 copy-start.3
  262.3 1.0 copy-start.4
  292.4 51.9 %all-to-all-start.3 = ((f32[8,4,128,128]{3,2,1,0:T(8,128)}), f32[8,4,128,128]{3,2,1,0:T(8,128)S(1)}, u32[]{:S(2)}, u32[]{:S(2)}) async-start(f32[8,4,128,128]{3,2,1,0:T(8,128)} %bitcast.12), calls=%async_computation.3 | async-start | bytes 4194304 | tf_op jit(solution)/shard_map/all_to_all | solution.py:536
  344.3 5.7 %copy-start.1 = (f32[64,32]{0,1:T(8,128)S(1)}, f32[64,32]{0,1:T(8,128)}, u32[]{:S(2)}) copy-start(f32[64,32]{0,1:T(8,128)} %param.26) | copy-start | bytes 24580
Sparse Core Ops, SparseCore 0:
  221.2 41.0 all-reduce.3

commit v3 on v2

--- a/solution.py
+++ b/solution.py
@@ -407,17 +407,10 @@
     slot_index = target * capacity + jnp.sum(earlier.astype(jnp.int32), axis=1)
     named = slot_index[None, :] == jnp.arange(slots, dtype=jnp.int32)[:, None]
     send_ids = blocks_here + jnp.sum(jnp.where(named, request_block[None, :] - blocks_here, 0), axis=1)
-    all_ids = lax.all_gather(send_ids, "tm", axis=0).reshape(owners, owners, capacity)
-    asked_ids = lax.dynamic_index_in_dim(all_ids, lax.axis_index("tm"), 1, False).reshape(-1)
-
-    outgoing = pl.pallas_call(
-        pick_kernel,
-        in_specs=[SCALARS, pl.BlockSpec(memory_space=pltpu.VMEM)],
-        out_specs=pl.BlockSpec(memory_space=pltpu.VMEM),
-        out_shape=struct(slots, rows_here, tile),
-        compiler_params=PARAMS,
-        name="pick_blocks",
-    )(asked_ids, sky_map)
+    asked_ids = lax.all_to_all(
+        send_ids.reshape(owners, capacity), "tm", split_axis=0, concat_axis=0, tiled=True
+    ).reshape(-1)
+
     packed = pl.pallas_call(
         sky_forward_kernel,
         grid=(groups // BATCH,),
@@ -432,7 +425,16 @@
     if parts > 1:
         packed = packed.reshape(groups, rows_here, parts, per_device).transpose(0, 2, 1, 3)
         packed = packed.reshape(devices, rows_here, per_device)
+    packed, asked_ids = lax.optimization_barrier((packed, asked_ids))
     columns = lax.all_to_all(packed, ("det", "tm"), split_axis=0, concat_axis=0, tiled=True)
+    outgoing = pl.pallas_call(
+        pick_kernel,
+        in_specs=[SCALARS, pl.BlockSpec(memory_space=pltpu.VMEM)],
+        out_specs=pl.BlockSpec(memory_space=pltpu.VMEM),
+        out_shape=struct(slots, rows_here, tile),
+        compiler_params=PARAMS,
+        name="pick_blocks",
+    )(asked_ids, sky_map)
     columns, outgoing = lax.optimization_barrier((columns, outgoing))
     columns = columns.reshape(total_rows, per_device)
     arrived = lax.all_to_all(

time: 358 us -> 348 us (0.972)
  blocking collectives: 115 us -> 0 us
  waiting for transfers between devices: 115 us -> 212 us
  starting transfers between devices: 19.5 us -> 25.2 us
    unnamed x1 -> x0, blocking collectives: 115 us -> none
    all_to_all x1, waiting for transfers between devices: 0.01 us -> 90.9 us  [local(): lax.all_to_all(packed, ('det', 'tm'), split_axis=0, concat_axis=0, tiled=...]
    all_to_all x0 -> x1, starting transfers between devices: none -> 7.25 us  [local(): lax.all_to_all(send_ids.reshape(owners, capacity), 'tm', split_axis=0, co...]
    all_to_all x1, waiting for transfers between devices: 27.7 us -> 33.9 us  [local(): lax.all_to_all(outgoing.reshape(owners, capacity, rows_here, tile), 'tm',...]
  transfers between devices with their start and end apart: 5 -> 6, of which waited for: 4 -> 5; matrix products, arithmetic and copies ran while one was open for 1% -> 0% of each run, Pallas kernels for 20% -> 24%
where the time goes in v3:
time: 348 us; the launch traced here: 346 us
  waiting for transfers between devices  212 us (61%)
  Pallas kernels  88 us (25%)
  starting transfers between devices  25.2 us (7%)
  between operations  13.5 us (4%)
  local copies, waits for them, and re-layouts  4.51 us (1%)
    all_to_all x1, waiting for transfers between devices, local(): lax.all_to_all(packed, ('det', 'tm'), split_axis=0, concat_axis=0, tiled=...  90.9 us
    psum x1, waiting for transfers between devices, local(): proj = lax.psum(proj, 'det')  40.4 us
    all_to_all x1, waiting for transfers between devices, local(): lax.all_to_all(returned.reshape(owners, capacity, rows_here, tile), 'tm',...  36.7 us
    all_to_all x1, waiting for transfers between devices, local(): lax.all_to_all(outgoing.reshape(owners, capacity, rows_here, tile), 'tm',...  33.9 us
    pallas_call x1, Pallas kernels, local(): pl.pallas_call(data_forward_kernel, grid=(time_groups // BATCH,), in_spec...  22 us
    pallas_call x1, Pallas kernels, local(): pl.pallas_call(data_backward_kernel, grid=(time_groups // BATCH,), in_spe...  19.2 us
    pallas_call x1, Pallas kernels, local(): pl.pallas_call(functools.partial(column_kernel, knee_sq=knee_sq), grid=(c...  13.7 us
    pallas_call x1, Pallas kernels, local(): pl.pallas_call(sky_forward_kernel, grid=(groups // BATCH,), in_specs=[who...  11.6 us
  transfers between devices with their start and end apart: 6, of which 5 were waited for; matrix products, arithmetic and copies ran while one was open for 0% of the time, Pallas kernels for 24%

profile of v3, /device:TPU:0, one launch (start us, length us, event | category | flops | bytes accessed | tf_op | source)
XLA Modules:
  0.0 346.4 jit_solution(16737952763847892096)
XLA Ops:
  6.5 0.0 copy-start
  6.5 0.9 convert_reduce_fusion
  7.4 0.7 multiply_add_fusion
  8.1 0.1 select_reduce_fusion
  8.2 0.7 add.33
  8.9 7.3 %all-to-all-start = ((s32[8,1,4]{2,1,0:T(1,128)}), s32[8,1,4]{2,1,0:T(1,128)S(1)}, u32[]{:S(2)}, u32[]{:S(2)}) async-start(s32[8,1,4]{2,1,0:T(1,128)} %bitcast.1), calls=%async_computation | async-start | bytes 8192 | tf_op jit(solution)/shard_map/all_to_all | solution.py:410
  16.2 11.6 %sky_forward.1 = f32[32,128,256]{2,1,0:T(8,128)} custom-call(f32[128,8192]{1,0:T(8,128)} %sky.3, bf16[32,256,256]{2,1,0:T(8,128)(2,1)} %constant.43.clone.high, bf16[32,256,256]{2,1,0:T(8,128)(2,1)} %constant.44.clone.low), custom_call_target="tpu_custom_call" | custom-call | tf_op jit(solution)/shard_map/sky_forward/pallas_call | solution.py:414
  27.8 0.0 all-to-all-done
  27.8 0.5 broadcast.30
  28.3 0.6 reduce.3
  29.0 0.1 reshape.49.ids
  29.0 6.2 %all-to-all-start.1 = ((f32[32,128,256]{2,1,0:T(8,128)}), f32[32,128,256]{2,1,0:T(8,128)}, u32[]{:S(2)}, u32[]{:S(2)}) async-start(f32[32,128,256]{2,1,0:T(8,128)} %sky_forward.1), calls=%async_computation.1 | async-start | bytes 8388608 | tf_op jit(solution)/shard_map/all_to_all | solution.py:429
  35.2 0.0 copy-start.2
  35.2 4.2 %pick_blocks.1 = f32[32,128,128]{2,1,0:T(8,128)} custom-call(s32[32]{0:T(128)S(1)} %reshape.49.ids, f32[128,8192]{1,0:T(8,128)} %sky.3), custom_call_target="tpu_custom_call" | custom-call | tf_op jit(solution)/shard_map/pick_blocks/pallas_call | solution.py:430
  39.4 90.9 %all-to-all-done.1 = f32[32,128,256]{2,1,0:T(8,128)} async-done(((f32[32,128,256]{2,1,0:T(8,128)}), f32[32,128,256]{2,1,0:T(8,128)}, u32[]{:S(2)}, u32[]{:S(2)}) %all-to-all-start.1) | async-done | bytes 4194336 | tf_op jit(solution)/shard_map/all_to_all | solution.py:429
  130.4 4.4 %all-to-all-start.2 = ((f32[8,4,128,128]{3,2,1,0:T(8,128)}), f32[8,4,128,128]{3,2,1,0:T(8,128)}, u32[]{:S(2)}, u32[]{:S(2)}) async-start(f32[8,4,128,128]{3,2,1,0:T(8,128)} %bitcast.3), calls=%async_computation.2 | async-start | bytes 4194304 | tf_op jit(solution)/shard_map/all_to_all | solution.py:440
  134.7 0.7 constant_dynamic-slice_fusion.col_sq
  135.5 0.0 copy-done.2
  135.5 13.7 %sky_columns.1 = f32[4096,256]{1,0:T(8,128)} custom-call(f32[4096,256]{1,0:T(8,128)} %bitcast.2.cols, f32[16,256,1]{2,1,0:T(8,128)S(1)} %copy-done.2, f32[1,256]{1,0:T(1,128)S(1)} %constant_dynamic-slice_fusion.col_sq, bf16[16,256,256]{2,1,0:T(8,128)(2,1)} %constant.47.clone.f_high, bf16[16,256,256]{2,1,0:T(8,128)(2,1)} %constant.48.clone.f_low, ...), custom_call_target="tpu_custom_call" | custom-call | tf_op jit(solution)/shard_map/sky_columns/pallas_call | solution.py:454
  149.2 33.9 %all-to-all-done.2 = f32[8,4,128,128]{3,2,1,0:T(8,128)} async-done(((f32[8,4,128,128]{3,2,1,0:T(8,128)}), f32[8,4,128,128]{3,2,1,0:T(8,128)}, u32[]{:S(2)}, u32[]{:S(2)}) %all-to-all-start.2) | async-done | bytes 2097184 | tf_op jit(solution)/shard_map/all_to_all | solution.py:440
  183.1 0.0 copy-start.10
  183.1 0.0 copy-start.8
  183.1 0.0 copy-start.5
  183.1 0.0 copy-start.6
  183.1 3.7 %all-to-all-start.3 = ((f32[32,128,256]{2,1,0:T(8,128)}), f32[32,128,256]{2,1,0:T(8,128)}, u32[]{:S(2)}, u32[]{:S(2)}) async-start(f32[32,128,256]{2,1,0:T(8,128)} %bitcast.25), calls=%async_computation.3 | async-start | bytes 8388608 | tf_op jit(solution)/shard_map/all_to_all | solution.py:466
  186.8 0.0 all-reduce.2.cloned.1.call-start
  186.9 0.0 copy-done.10
  186.9 0.1 copy.32.loading
  187.0 0.0 copy-done
  187.0 0.0 copy-done.8
  187.0 0.3 convolution_bitcast_fusion.1.white
  187.3 0.0 copy-done.5
  187.3 0.0 copy-done.6
  187.3 0.0 copy-start.7
  187.3 0.0 copy-start.9
  187.3 22.0 %data_forward.1 = (f32[32,64,256]{2,1,0:T(8,128)S(1)}, f32[32,16,256]{2,1,0:T(8,128)}) custom-call(s32[64,64]{1,0:T(8,128)S(1)} %copy-done.6, s32[16]{0:T(128)S(1)} %get-tuple-element.25.slots, f32[32,128,128]{2,1,0:T(8,128)} %bitcast.4.arrived, f32[64,8192]{1,0:T(8,128)} %data.1, f32[128,128]{1,0:T(8,128)S(1)} %copy-done.5, ...), custom_call_target="tpu_custom_call" | custom-call | tf_op jit(solution)/shard_map/data_forward/pallas_call | solution.py:483
  209.3 0.0 copy-start.3
  209.3 1.3 copy-done.3
  210.6 0.0 all-reduce.2.cloned.1.call-update
  210.7 0.0 copy-done.7
  210.7 0.0 copy-done.9
  210.7 0.6 convolution_bitcast_fusion.coupling
  211.3 40.4 %all-reduce.2.cloned.1.call-done.proj = f32[32,16,256]{2,1,0:T(8,128)} async-done(((f32[32,16,256]{2,1,0:T(8,128)}), f32[32,16,256]{2,1,0:T(8,128)}) %all-reduce.2.cloned.1.call-update) | async-done | bytes 524304 | tf_op jit(solution)/shard_map/psum | solution.py:510
  251.6 0.0 copy-start.4
  251.7 1.0 copy-done.4
  252.7 19.2 %data_backward.1 = f32[32,128,128]{2,1,0:T(8,128)} custom-call(s32[64,64]{1,0:T(8,128)S(1)} %copy-done.6, s32[16]{0:T(128)S(1)} %get-tuple-element.25.slots, f32[32,64,256]{2,1,0:T(8,128)} %copy-done.3, f32[32,16,256]{2,1,0:T(8,128)S(1)} %copy-done.4, f32[2,16,16,256]{3,2,1,0:T(8,128)S(1)} %convolution_bitcast_fusion.coupling, f32[128,128]{1,0:T(8,128)S(1)} %copy-done.5, ...), custom_call_target="tpu_custom_call" | custom-call | tf_op jit(solution)/shard_map/data_backward/pallas_call | solution.py:512
  271.9 10.1 %all-to-all-done.3.spectrum = f32[32,128,256]{2,1,0:T(8,128)} async-done(((f32[32,128,256]{2,1,0:T(8,128)}), f32[32,128,256]{2,1,0:T(8,128)}, u32[]{:S(2)}, u32[]{:S(2)}) %all-to-all-start.3) | async-done | bytes 4194336 | tf_op jit(solution)/shard_map/all_to_all | solution.py:466
  282.0 3.6 %all-to-all-start.4 = ((f32[8,4,128,128]{3,2,1,0:T(8,128)}), f32[8,4,128,128]{3,2,1,0:T(8,128)S(1)}, u32[]{:S(2)}, u32[]{:S(2)}) async-start(f32[8,4,128,128]{3,2,1,0:T(8,128)} %bitcast.12), calls=%async_computation.4 | async-start | bytes 4194304 | tf_op jit(solution)/shard_map/all_to_all | solution.py:538
  285.6 11.6 %sky_backward.1.base = f32[128,8192]{1,0:T(8,128)} custom-call(f32[32,128,256]{2,1,0:T(8,128)} %all-to-all-done.3.spectrum, bf16[32,256,256]{2,1,0:T(8,128)(2,1)} %constant.45.clone.high, bf16[32,256,256]{2,1,0:T(8,128)(2,1)} %constant.46.clone.low), custom_call_target="tpu_custom_call" | custom-call | tf_op jit(solution)/shard_map/sky_backward/pallas_call | solution.py:542
  297.1 36.7 %all-to-all-done.4 = f32[8,4,128,128]{3,2,1,0:T(8,128)S(1)} async-done(((f32[8,4,128,128]{3,2,1,0:T(8,128)}), f32[8,4,128,128]{3,2,1,0:T(8,128)S(1)}, u32[]{:S(2)}, u32[]{:S(2)}) %all-to-all-start.4) | async-done | bytes 2097184 | tf_op jit(solution)/shard_map/all_to_all | solution.py:538
  333.8 0.0 copy-start.1
  333.8 5.7 %sky_finish.1 = f32[128,8192]{1,0:T(8,128)} custom-call(s32[32]{0:T(128)S(1)} %reshape.49.ids, f32[128,8192]{1,0:T(8,128)} %sky_backward.1.base, f32[32,128,128]{2,1,0:T(8,128)S(1)} %bitcast.24), custom_call_target="tpu_custom_call" | custom-call | tf_op jit(solution)/shard_map/sky_finish/pallas_call | solution.py:554
  339.6 0.0 copy-done.1
  (1 shorter events, 0.0 us)
Async XLA Ops:
  6.5 180.4 %copy-start = (f32[64,32]{0,1:T(8,128)S(1)}, f32[64,32]{0,1:T(8,128)}, u32[]{:S(2)}) copy-start(f32[64,32]{0,1:T(8,128)} %param.26) | copy-start | bytes 24580
  8.9 18.9 %all-to-all-start = ((s32[8,1,4]{2,1,0:T(1,128)}), s32[8,1,4]{2,1,0:T(1,128)S(1)}, u32[]{:S(2)}, u32[]{:S(2)}) async-start(s32[8,1,4]{2,1,0:T(1,128)} %bitcast.1), calls=%async_computation | async-start | bytes 8192 | tf_op jit(solution)/shard_map/all_to_all | solution.py:410
  29.0 101.3 %all-to-all-start.1 = ((f32[32,128,256]{2,1,0:T(8,128)}), f32[32,128,256]{2,1,0:T(8,128)}, u32[]{:S(2)}, u32[]{:S(2)}) async-start(f32[32,128,256]{2,1,0:T(8,128)} %sky_forward.1), calls=%async_computation.1 | async-start | bytes 8388608 | tf_op jit(solution)/shard_map/all_to_all | solution.py:429
  35.2 100.2 %copy-start.2 = (f32[16,256,1]{2,1,0:T(8,128)S(1)}, f32[16,256,1]{2,1,0:T(8,128)}, u32[]{:S(2)}) copy-start(f32[16,256,1]{2,1,0:T(8,128)} %constant.52.clone.row_sq) | copy-start | bytes 49156
  130.4 52.7 %all-to-all-start.2 = ((f32[8,4,128,128]{3,2,1,0:T(8,128)}), f32[8,4,128,128]{3,2,1,0:T(8,128)}, u32[]{:S(2)}, u32[]{:S(2)}) async-start(f32[8,4,128,128]{3,2,1,0:T(8,128)} %bitcast.3), calls=%async_computation.2 | async-start | bytes 4194304 | tf_op jit(solution)/shard_map/all_to_all | solution.py:440
  183.1 3.8 %copy-start.10 = (f32[64,16]{0,1:T(8,128)S(1)}, f32[64,16]{0,1:T(8,128)}, u32[]{:S(2)}) copy-start(f32[64,16]{0,1:T(8,128)} %param.27) | copy-start | bytes 12292
  183.1 3.9 %copy-start.8 = (f32[32,2,256]{2,0,1:T(8,128)S(1)}, f32[32,2,256]{2,0,1:T(8,128)}, u32[]{:S(2)}) copy-start(f32[32,2,256]{2,0,1:T(8,128)} %constant.53.clone) | copy-start | bytes 196612
  183.1 4.2 %copy-start.5 = (f32[128,128]{1,0:T(8,128)S(1)}, f32[128,128]{1,0:T(8,128)}, u32[]{:S(2)}) copy-start(f32[128,128]{1,0:T(8,128)} %beam.3) | copy-start | bytes 196612
  183.1 4.2 %copy-start.6 = (s32[64,64]{1,0:T(8,128)S(1)}, s32[64,64]{1,0:T(8,128)}, u32[]{:S(2)}) copy-start(s32[64,64]{1,0:T(8,128)} %pointing.3) | copy-start | bytes 49156
  183.1 98.9 %all-to-all-start.3 = ((f32[32,128,256]{2,1,0:T(8,128)}), f32[32,128,256]{2,1,0:T(8,128)}, u32[]{:S(2)}, u32[]{:S(2)}) async-start(f32[32,128,256]{2,1,0:T(8,128)} %bitcast.25), calls=%async_computation.3 | async-start | bytes 8388608 | tf_op jit(solution)/shard_map/all_to_all | solution.py:466
  186.8 64.8 %all-reduce.2.cloned.1.call-start = ((), (), s32[]{:S(2)}) async-start(), calls=%async_computation.5 | async-start | bytes 1048576 | tf_op jit(solution)/shard_map/psum | solution.py:510
  187.3 23.4 %copy-start.7 = (f32[32,16,16]{0,2,1:T(8,128)S(1)}, f32[32,16,16]{0,2,1:T(8,128)}, u32[]{:S(2)}) copy-start(f32[32,16,16]{0,2,1:T(8,128)} %param.28) | copy-start | bytes 98308
  187.3 23.3 %copy-start.9 = (f32[32,2,256,1]{2,0,3,1:T(8,128)S(1)}, f32[32,2,256,1]{2,0,3,1:T(8,128)}, u32[]{:S(2)}) copy-start(f32[32,2,256,1]{2,0,3,1:T(8,128)} %constant.56) | copy-start | bytes 196612
  209.3 1.3 copy-start.3
  251.6 1.0 copy-start.4
  282.0 51.9 %all-to-all-start.4 = ((f32[8,4,128,128]{3,2,1,0:T(8,128)}), f32[8,4,128,128]{3,2,1,0:T(8,128)S(1)}, u32[]{:S(2)}, u32[]{:S(2)}) async-start(f32[8,4,128,128]{3,2,1,0:T(8,128)} %bitcast.12), calls=%async_computation.4 | async-start | bytes 4194304 | tf_op jit(solution)/shard_map/all_to_all | solution.py:538
  333.8 5.7 %copy-start.1 = (f32[64,32]{0,1:T(8,128)S(1)}, f32[64,32]{0,1:T(8,128)}, u32[]{:S(2)}) copy-start(f32[64,32]{0,1:T(8,128)} %param.26) | copy-start | bytes 24580
Sparse Core Ops, SparseCore 0:
  210.8 40.8 all-reduce.1

commit v4 on v3

--- a/solution.py
+++ b/solution.py
@@ -72,7 +72,11 @@
 
 def multiply(left, right, dims=(((1,), (0,)), ((), ()))):
     dot = functools.partial(lax.dot_general, dimension_numbers=dims, preferred_element_type=F32)
-    return dot(left[0], right[0]) + (dot(left[1], right[0]) + dot(left[0], right[1]))
+    if dims[0][0] == (0,):
+        return dot(left[0], right[0]) + (dot(left[1], right[0]) + dot(left[0], right[1]))
+    rows = left[0].shape[0]
+    both = dot(jnp.concatenate(left, axis=0), right[0])
+    return both[:rows] + (both[rows:] + dot(left[0], right[1]))
 
 
 def forward_stage(load, start, step, count):
@@ -355,6 +359,7 @@
 
 
 PARAMS = pltpu.CompilerParams(vmem_limit_bytes=LIMIT)
+SKY_PARAMS = pltpu.CompilerParams(vmem_limit_bytes=LIMIT // 2)
 
 
 def struct(*shape):
@@ -418,7 +423,7 @@
         out_specs=pl.BlockSpec((BATCH, rows_here, wide), lambda g: (g, 0, 0)),
         out_shape=struct(groups, rows_here, wide),
         scratch_shapes=[pltpu.VMEM((groups, rows_here, wide), F32)],
-        compiler_params=PARAMS,
+        compiler_params=SKY_PARAMS,
         name="sky_forward",
     )(sky_map, *row_forward)
     parts = wide // per_device
@@ -546,7 +551,7 @@
         out_specs=pl.BlockSpec((rows_here, map_cols), lambda g: (0, 0)),
         out_shape=struct(rows_here, map_cols),
         scratch_shapes=[pltpu.VMEM((groups, rows_here, wide), F32)],
-        compiler_params=PARAMS,
+        compiler_params=SKY_PARAMS,
         name="sky_backward",
     )(spectrum, *row_backward)
 
@@ -561,7 +566,7 @@
         ],
         out_specs=pl.BlockSpec((chunk, map_cols), lambda g: (g, 0)),
         out_shape=struct(rows_here, map_cols),
-        compiler_params=PARAMS,
+        compiler_params=SKY_PARAMS,
         name="sky_finish",
     )(asked_ids, base, delivered)
 

time: 348 us -> 350 us (level)
  local copies, waits for them, and re-layouts: 4.51 us -> 21.7 us
  Pallas kernels: 88 us -> 73.5 us
    unnamed x23 -> x39, local copies, waits for them, and re-layouts: 2.5 us -> 19.7 us
    pallas_call x1, Pallas kernels: 11.6 us -> 4.61 us  [local(): pl.pallas_call(sky_forward_kernel, grid=(groups // BATCH,), in_specs=[who...]
    pallas_call x1, Pallas kernels: 11.6 us -> 8.06 us  [local(): pl.pallas_call(sky_backward_kernel, grid=(groups // BATCH,), in_specs=[sl...]
  transfers between devices with their start and end apart: 6 -> 6, of which waited for: 5 -> 5; matrix products, arithmetic and copies ran while one was open for 0% -> 0% of each run, Pallas kernels for 24% -> 20%
where the time goes in v4:
time: 350 us; the launch traced here: 349 us
  waiting for transfers between devices  212 us (61%)
  Pallas kernels  73.5 us (21%)
  starting transfers between devices  25.2 us (7%)
  local copies, waits for them, and re-layouts  21.7 us (6%)
  between operations  13.6 us (4%)
    all_to_all x1, waiting for transfers between devices, local(): lax.all_to_all(packed, ('det', 'tm'), split_axis=0, concat_axis=0, tiled=...  90.9 us
    psum x1, waiting for transfers between devices, local(): proj = lax.psum(proj, 'det')  42.4 us
    all_to_all x1, waiting for transfers between devices, local(): lax.all_to_all(outgoing.reshape(owners, capacity, rows_here, tile), 'tm',...  33.9 us
    all_to_all x1, waiting for transfers between devices, local(): lax.all_to_all(returned.reshape(owners, capacity, rows_here, tile), 'tm',...  33.8 us
    pallas_call x1, Pallas kernels, local(): pl.pallas_call(data_forward_kernel, grid=(time_groups // BATCH,), in_spec...  19.9 us
    unnamed x39, local copies, waits for them, and re-layouts  19.7 us
    pallas_call x1, Pallas kernels, local(): pl.pallas_call(data_backward_kernel, grid=(time_groups // BATCH,), in_spe...  18.8 us
    pallas_call x1, Pallas kernels, local(): pl.pallas_call(functools.partial(column_kernel, knee_sq=knee_sq), grid=(c...  13.8 us
  transfers between devices with their start and end apart: 6, of which 5 were waited for; matrix products, arithmetic and copies ran while one was open for 0% of the time, Pallas kernels for 20%

profile of v4, /device:TPU:0, one launch (start us, length us, event | category | flops | bytes accessed | tf_op | source)
XLA Modules:
  0.0 348.7 jit_solution(5343034923429609840)
XLA Ops:
  6.5 0.0 copy-start
  6.5 0.9 convert_reduce_fusion
  7.4 0.7 multiply_add_fusion
  8.1 0.1 select_reduce_fusion
  8.2 0.7 add.33
  8.9 7.3 %all-to-all-start = ((s32[8,1,4]{2,1,0:T(1,128)}), s32[8,1,4]{2,1,0:T(1,128)S(1)}, u32[]{:S(2)}, u32[]{:S(2)}) async-start(s32[8,1,4]{2,1,0:T(1,128)} %bitcast.1), calls=%async_computation | async-start | bytes 8192 | tf_op jit(solution)/shard_map/all_to_all | solution.py:415
  16.2 0.0 copy-start.2
  16.2 2.2 copy-done.2
  18.3 0.0 copy-start.3
  18.3 2.2 copy-done.3
  20.5 0.0 copy-start.4
  20.5 2.2 copy-done.4
  22.7 4.6 %sky_forward.1 = f32[32,128,256]{2,1,0:T(8,128)S(1)} custom-call(f32[128,8192]{1,0:T(8,128)S(1)} %copy-done.2, bf16[32,256,256]{2,1,0:T(8,128)(2,1)S(1)} %copy-done.3, bf16[32,256,256]{2,1,0:T(8,128)(2,1)S(1)} %copy-done.4), custom_call_target="tpu_custom_call" | custom-call | tf_op jit(solution)/shard_map/sky_forward/pallas_call | solution.py:419
  27.3 0.0 copy-start.5
  27.3 2.0 copy-done.5
  29.4 0.0 all-to-all-done
  29.4 0.5 broadcast.30
  29.9 0.6 reduce.3
  30.6 0.1 reshape.49.ids
  30.6 6.2 %all-to-all-start.1 = ((f32[32,128,256]{2,1,0:T(8,128)}), f32[32,128,256]{2,1,0:T(8,128)}, u32[]{:S(2)}, u32[]{:S(2)}) async-start(f32[32,128,256]{2,1,0:T(8,128)} %copy-done.5), calls=%async_computation.1 | async-start | bytes 8388608 | tf_op jit(solution)/shard_map/all_to_all | solution.py:434
  36.8 0.0 copy-start.10
  36.8 4.2 %pick_blocks.1 = f32[32,128,128]{2,1,0:T(8,128)} custom-call(s32[32]{0:T(128)S(1)} %reshape.49.ids, f32[128,8192]{1,0:T(8,128)} %sky.3), custom_call_target="tpu_custom_call" | custom-call | tf_op jit(solution)/shard_map/pick_blocks/pallas_call | solution.py:435
  41.0 90.9 %all-to-all-done.1 = f32[32,128,256]{2,1,0:T(8,128)} async-done(((f32[32,128,256]{2,1,0:T(8,128)}), f32[32,128,256]{2,1,0:T(8,128)}, u32[]{:S(2)}, u32[]{:S(2)}) %all-to-all-start.1) | async-done | bytes 4194336 | tf_op jit(solution)/shard_map/all_to_all | solution.py:434
  132.0 4.4 %all-to-all-start.2 = ((f32[8,4,128,128]{3,2,1,0:T(8,128)}), f32[8,4,128,128]{3,2,1,0:T(8,128)}, u32[]{:S(2)}, u32[]{:S(2)}) async-start(f32[8,4,128,128]{3,2,1,0:T(8,128)} %bitcast.3), calls=%async_computation.2 | async-start | bytes 4194304 | tf_op jit(solution)/shard_map/all_to_all | solution.py:445
  136.3 0.7 constant_dynamic-slice_fusion.col_sq
  137.0 0.0 copy-done.10
  137.0 13.8 %sky_columns.1 = f32[4096,256]{1,0:T(8,128)} custom-call(f32[4096,256]{1,0:T(8,128)} %bitcast.2.cols, f32[16,256,1]{2,1,0:T(8,128)S(1)} %copy-done.10, f32[1,256]{1,0:T(1,128)S(1)} %constant_dynamic-slice_fusion.col_sq, bf16[16,256,256]{2,1,0:T(8,128)(2,1)} %constant.47.clone.f_high, bf16[16,256,256]{2,1,0:T(8,128)(2,1)} %constant.48.clone.f_low, ...), custom_call_target="tpu_custom_call" | custom-call | tf_op jit(solution)/shard_map/sky_columns/pallas_call | solution.py:459
  150.8 33.9 %all-to-all-done.2 = f32[8,4,128,128]{3,2,1,0:T(8,128)} async-done(((f32[8,4,128,128]{3,2,1,0:T(8,128)}), f32[8,4,128,128]{3,2,1,0:T(8,128)}, u32[]{:S(2)}, u32[]{:S(2)}) %all-to-all-start.2) | async-done | bytes 2097184 | tf_op jit(solution)/shard_map/all_to_all | solution.py:445
  184.7 0.0 copy-start.18
  184.7 0.0 copy-start.16
  184.7 0.0 copy-start.13
  184.7 0.0 copy-start.14
  184.7 3.7 %all-to-all-start.3 = ((f32[32,128,256]{2,1,0:T(8,128)}), f32[32,128,256]{2,1,0:T(8,128)}, u32[]{:S(2)}, u32[]{:S(2)}) async-start(f32[32,128,256]{2,1,0:T(8,128)} %bitcast.25), calls=%async_computation.3 | async-start | bytes 8388608 | tf_op jit(solution)/shard_map/all_to_all | solution.py:471
  188.4 0.0 all-reduce.2.cloned.1.call-start
  188.5 0.0 copy-done.18
  188.5 0.1 copy.32.loading
  188.6 0.0 copy-done
  188.6 0.0 copy-done.16
  188.6 0.3 convolution_bitcast_fusion.1.white
  188.9 0.0 copy-done.13
  188.9 0.0 copy-done.14
  188.9 0.0 copy-start.15
  188.9 0.0 copy-start.17
  188.9 19.9 %data_forward.1 = (f32[32,64,256]{2,1,0:T(8,128)S(1)}, f32[32,16,256]{2,1,0:T(8,128)}) custom-call(s32[64,64]{1,0:T(8,128)S(1)} %copy-done.14, s32[16]{0:T(128)S(1)} %get-tuple-element.25.slots, f32[32,128,128]{2,1,0:T(8,128)} %bitcast.4.arrived, f32[64,8192]{1,0:T(8,128)} %data.1, f32[128,128]{1,0:T(8,128)S(1)} %copy-done.13, ...), custom_call_target="tpu_custom_call" | custom-call | tf_op jit(solution)/shard_map/data_forward/pallas_call | solution.py:488
  208.9 1.3 copy-done.11
  210.2 0.0 all-reduce.2.cloned.1.call-update
  210.2 0.0 copy-done.15
  210.2 0.0 copy-done.17
  210.3 0.6 convolution_bitcast_fusion.coupling
  210.8 42.4 %all-reduce.2.cloned.1.call-done.proj = f32[32,16,256]{2,1,0:T(8,128)} async-done(((f32[32,16,256]{2,1,0:T(8,128)}), f32[32,16,256]{2,1,0:T(8,128)}) %all-reduce.2.cloned.1.call-update) | async-done | bytes 524304 | tf_op jit(solution)/shard_map/psum | solution.py:515
  253.3 1.0 copy-done.12
  254.3 18.8 %data_backward.1 = f32[32,128,128]{2,1,0:T(8,128)} custom-call(s32[64,64]{1,0:T(8,128)S(1)} %copy-done.14, s32[16]{0:T(128)S(1)} %get-tuple-element.25.slots, f32[32,64,256]{2,1,0:T(8,128)} %copy-done.11, f32[32,16,256]{2,1,0:T(8,128)S(1)} %copy-done.12, f32[2,16,16,256]{3,2,1,0:T(8,128)S(1)} %convolution_bitcast_fusion.coupling, f32[128,128]{1,0:T(8,128)S(1)} %copy-done.13, ...), custom_call_target="tpu_custom_call" | custom-call | tf_op jit(solution)/shard_map/data_backward/pallas_call | solution.py:517
  273.1 10.5 %all-to-all-done.3.spectrum = f32[32,128,256]{2,1,0:T(8,128)} async-done(((f32[32,128,256]{2,1,0:T(8,128)}), f32[32,128,256]{2,1,0:T(8,128)}, u32[]{:S(2)}, u32[]{:S(2)}) %all-to-all-start.3) | async-done | bytes 4194336 | tf_op jit(solution)/shard_map/all_to_all | solution.py:471
  283.6 3.6 %all-to-all-start.4 = ((f32[8,4,128,128]{3,2,1,0:T(8,128)}), f32[8,4,128,128]{3,2,1,0:T(8,128)S(1)}, u32[]{:S(2)}, u32[]{:S(2)}) async-start(f32[8,4,128,128]{3,2,1,0:T(8,128)} %bitcast.12), calls=%async_computation.4 | async-start | bytes 4194304 | tf_op jit(solution)/shard_map/all_to_all | solution.py:543
  287.2 0.0 copy-start.8
  287.2 2.2 copy-done.8
  289.4 2.2 copy-done.9
  291.6 8.1 %sky_backward.1.base = f32[128,8192]{1,0:T(8,128)S(1)} custom-call(f32[32,128,256]{2,1,0:T(8,128)} %all-to-all-done.3.spectrum, bf16[32,256,256]{2,1,0:T(8,128)(2,1)S(1)} %copy-done.8, bf16[32,256,256]{2,1,0:T(8,128)(2,1)S(1)} %copy-done.9), custom_call_target="tpu_custom_call" | custom-call | tf_op jit(solution)/shard_map/sky_backward/pallas_call | solution.py:547
  299.6 0.0 copy-start.6
  299.6 2.0 copy-done.6
  301.6 33.8 %all-to-all-done.4 = f32[8,4,128,128]{3,2,1,0:T(8,128)S(1)} async-done(((f32[8,4,128,128]{3,2,1,0:T(8,128)}), f32[8,4,128,128]{3,2,1,0:T(8,128)S(1)}, u32[]{:S(2)}, u32[]{:S(2)}) %all-to-all-start.4) | async-done | bytes 2097184 | tf_op jit(solution)/shard_map/all_to_all | solution.py:543
  335.4 2.2 copy-done.7
  337.6 4.2 %sky_finish.1 = f32[128,8192]{1,0:T(8,128)} custom-call(s32[32]{0:T(128)S(1)} %reshape.49.ids, f32[128,8192]{1,0:T(8,128)S(1)} %copy-done.7, f32[32,128,128]{2,1,0:T(8,128)S(1)} %bitcast.24), custom_call_target="tpu_custom_call" | custom-call | tf_op jit(solution)/shard_map/sky_finish/pallas_call | solution.py:559
  341.8 0.0 copy-done.1
  (6 shorter events, 0.0 us)
Async XLA Ops:
  6.5 182.0 %copy-start = (f32[64,32]{0,1:T(8,128)S(1)}, f32[64,32]{0,1:T(8,128)}, u32[]{:S(2)}) copy-start(f32[64,32]{0,1:T(8,128)} %param.26) | copy-start | bytes 24580
  8.9 20.5 %all-to-all-start = ((s32[8,1,4]{2,1,0:T(1,128)}), s32[8,1,4]{2,1,0:T(1,128)S(1)}, u32[]{:S(2)}, u32[]{:S(2)}) async-start(s32[8,1,4]{2,1,0:T(1,128)} %bitcast.1), calls=%async_computation | async-start | bytes 8192 | tf_op jit(solution)/shard_map/all_to_all | solution.py:415
  16.2 2.2 copy-start.2
  18.3 2.2 copy-start.3
  20.5 2.2 copy-start.4
  27.3 2.0 copy-start.5
  30.6 101.3 %all-to-all-start.1 = ((f32[32,128,256]{2,1,0:T(8,128)}), f32[32,128,256]{2,1,0:T(8,128)}, u32[]{:S(2)}, u32[]{:S(2)}) async-start(f32[32,128,256]{2,1,0:T(8,128)} %copy-done.5), calls=%async_computation.1 | async-start | bytes 8388608 | tf_op jit(solution)/shard_map/all_to_all | solution.py:434
  36.8 100.2 %copy-start.10 = (f32[16,256,1]{2,1,0:T(8,128)S(1)}, f32[16,256,1]{2,1,0:T(8,128)}, u32[]{:S(2)}) copy-start(f32[16,256,1]{2,1,0:T(8,128)} %constant.52.clone.row_sq) | copy-start | bytes 49156
  132.0 52.7 %all-to-all-start.2 = ((f32[8,4,128,128]{3,2,1,0:T(8,128)}), f32[8,4,128,128]{3,2,1,0:T(8,128)}, u32[]{:S(2)}, u32[]{:S(2)}) async-start(f32[8,4,128,128]{3,2,1,0:T(8,128)} %bitcast.3), calls=%async_computation.2 | async-start | bytes 4194304 | tf_op jit(solution)/shard_map/all_to_all | solution.py:445
  184.7 3.8 %copy-start.18 = (f32[64,16]{0,1:T(8,128)S(1)}, f32[64,16]{0,1:T(8,128)}, u32[]{:S(2)}) copy-start(f32[64,16]{0,1:T(8,128)} %param.27) | copy-start | bytes 12292
  184.7 3.9 %copy-start.16 = (f32[32,2,256]{2,0,1:T(8,128)S(1)}, f32[32,2,256]{2,0,1:T(8,128)}, u32[]{:S(2)}) copy-start(f32[32,2,256]{2,0,1:T(8,128)} %constant.53.clone) | copy-start | bytes 196612
  184.7 4.2 %copy-start.13 = (f32[128,128]{1,0:T(8,128)S(1)}, f32[128,128]{1,0:T(8,128)}, u32[]{:S(2)}) copy-start(f32[128,128]{1,0:T(8,128)} %beam.3) | copy-start | bytes 196612
  184.7 4.2 %copy-start.14 = (s32[64,64]{1,0:T(8,128)S(1)}, s32[64,64]{1,0:T(8,128)}, u32[]{:S(2)}) copy-start(s32[64,64]{1,0:T(8,128)} %pointing.3) | copy-start | bytes 49156
  184.7 98.9 %all-to-all-start.3 = ((f32[32,128,256]{2,1,0:T(8,128)}), f32[32,128,256]{2,1,0:T(8,128)}, u32[]{:S(2)}, u32[]{:S(2)}) async-start(f32[32,128,256]{2,1,0:T(8,128)} %bitcast.25), calls=%async_computation.3 | async-start | bytes 8388608 | tf_op jit(solution)/shard_map/all_to_all | solution.py:471
  188.4 64.9 %all-reduce.2.cloned.1.call-start = ((), (), s32[]{:S(2)}) async-start(), calls=%async_computation.5 | async-start | bytes 1048576 | tf_op jit(solution)/shard_map/psum | solution.py:515
  188.9 21.3 %copy-start.15 = (f32[32,16,16]{0,2,1:T(8,128)S(1)}, f32[32,16,16]{0,2,1:T(8,128)}, u32[]{:S(2)}) copy-start(f32[32,16,16]{0,2,1:T(8,128)} %param.28) | copy-start | bytes 98308
  188.9 21.3 %copy-start.17 = (f32[32,2,256,1]{2,0,3,1:T(8,128)S(1)}, f32[32,2,256,1]{2,0,3,1:T(8,128)}, u32[]{:S(2)}) copy-start(f32[32,2,256,1]{2,0,3,1:T(8,128)} %constant.56) | copy-start | bytes 196612
  208.9 1.3 copy-start.11
  253.3 1.0 copy-start.12
  283.6 51.9 %all-to-all-start.4 = ((f32[8,4,128,128]{3,2,1,0:T(8,128)}), f32[8,4,128,128]{3,2,1,0:T(8,128)S(1)}, u32[]{:S(2)}, u32[]{:S(2)}) async-start(f32[8,4,128,128]{3,2,1,0:T(8,128)} %bitcast.12), calls=%async_computation.4 | async-start | bytes 4194304 | tf_op jit(solution)/shard_map/all_to_all | solution.py:543
  287.2 2.2 copy-start.8
  289.4 2.2 copy-start.9
  299.6 2.0 copy-start.6
  335.4 6.4 %copy-start.1 = (f32[64,32]{0,1:T(8,128)S(1)}, f32[64,32]{0,1:T(8,128)}, u32[]{:S(2)}) copy-start(f32[64,32]{0,1:T(8,128)} %param.26) | copy-start | bytes 24580
  335.4 2.2 copy-start.7
Sparse Core Ops, SparseCore 0:
  210.4 42.8 all-reduce.1
